TPU v7x, 256 devices: a whole 4x4x8 slice. The times are simulated.
256 devices in a mesh: sx: 4 (over x_lo, core), sy: 2 (over x_hi), fsdp: 32 (over z, y).
Axes of the slice: x: 4 (x_hi: 2, x_lo: 2; x = x_hi * 2 + x_lo), y: 4, z: 8, core: 2. Of those that a mesh axis runs over, the one named last changes fastest.
Arguments:
- x_code: bfloat16 [32, 32, 32, 1536], P('fsdp', 'sx', 'sy'), may hold values from -6 to 6
- x_exp: int32 [32, 32, 32, 12], P('fsdp', 'sx', 'sy'), may hold values from -2 to 2
- dw_kernel: float32 [7, 7, 1536], replicated, may hold values from -1.2 to 1.2
- dw_bias: float32 [1536], replicated, may hold values from -4 to 4
- ln_gain: float32 [1536], replicated, may hold values from 0.1 to 1.9
- ln_bias: float32 [1536], replicated, may hold values from -3 to 3
- w_up: bfloat16 [1536, 3072], P('fsdp'), may hold values from -0.15625 to 0.15625
- b_up: float32 [3072], replicated, may hold values from -3 to 3
- w_down: bfloat16 [3072, 1536], P(None, 'fsdp'), may hold values from -0.109375 to 0.109375
- b_down: float32 [1536], replicated, may hold values from -3 to 3
- layer_scale: float32 [1536], replicated, may hold values from 0.3 to 1.5
- cotangent: bfloat16 [32, 32, 32, 1536], P('fsdp', 'sx', 'sy'), may hold values from -6 to 6
Outputs:
- block_out: bfloat16 [32, 32, 32, 1536], P('fsdp', 'sx', 'sy')
- grad_input: bfloat16 [32, 32, 32, 1536], P('fsdp', 'sx', 'sy')
- grad_kernel: float32 [7, 7, 1536], replicated
- grad_gain: float32 [1536], replicated
- grad_scale: float32 [1536], replicated
All inputs are finite; a program needn't handle non-finite values.
Results may differ from a plain program's by a relative error of at most 0.006.
Values may be sent and summed in bfloat16 or wider, within the bound.
A program may use at most 192 MiB of HBM per device.

v0:
```python
import jax
import jax.numpy as jnp
from jax import lax
from jax.sharding import PartitionSpec as P

CG = 128
KW = 7


def with_halo(shard, sides, width):
    for axis, dim in sides:
        devices, length = (lax.axis_size(axis), shard.shape[dim])
        up = [(i, (i + 1) % devices) for i in range(devices - 1)]
        down = [(j, i) for i, j in up]
        last = lax.slice_in_dim(shard, length - width, length, axis=dim)
        initial = lax.slice_in_dim(shard, 0, width, axis=dim)
        before = lax.ppermute(last, axis, up)
        after = lax.ppermute(initial, axis, down)
        shard = jnp.concatenate([before, shard, after], axis=dim)
    return shard


def gelu_tanh(v):
    return jax.nn.gelu(v, approximate=True)


def on_device(
    x_code,
    x_exp,
    dw_kernel,
    dw_bias,
    ln_gain,
    ln_bias,
    w_up,
    b_up,
    w_down,
    b_down,
    layer_scale,
    cotangent,
):
    code = x_code[0]
    rows, cols, chans = code.shape
    factor = jnp.exp2(x_exp[0].astype(jnp.float32))
    grouped = code.astype(jnp.float32).reshape(rows, cols, chans // CG, CG) * factor[..., None]
    scaled = grouped.reshape(rows, cols, chans).astype(jnp.bfloat16)
    up_full, down_full = (
        lax.all_gather(w_up, "fsdp", axis=0, tiled=True),
        lax.all_gather(w_down, "fsdp", axis=1, tiled=True),
    )
    padded_x = with_halo(scaled[None], (("sx", 1), ("sy", 2)), 3)[0].astype(jnp.float32)
    conv = jnp.zeros((rows, cols, chans), jnp.float32) + dw_bias
    for i in range(KW):
        for j in range(KW):
            conv = conv + dw_kernel[i, j] * padded_x[i : i + rows, j : j + cols]
    mean_val = jnp.mean(conv, axis=-1, keepdims=True)
    centred = conv - mean_val
    rstd = lax.rsqrt(jnp.mean(centred * centred, axis=-1, keepdims=True) + 1e-06)
    normed = centred * rstd
    ln_out = (normed * ln_gain + ln_bias).astype(jnp.bfloat16).reshape(rows * cols, chans)
    pre = jnp.dot(ln_out, up_full, preferred_element_type=jnp.float32) + b_up
    act, gelu_back = jax.vjp(gelu_tanh, pre)
    mlp = jnp.dot(act.astype(jnp.bfloat16), down_full, preferred_element_type=jnp.float32) + b_down
    mlp = mlp.reshape(rows, cols, chans)
    block_out = (scaled.astype(jnp.float32) + layer_scale * mlp).astype(jnp.bfloat16)
    grad_f = cotangent[0].astype(jnp.float32)
    scale_term = jnp.sum(grad_f * mlp, axis=(0, 1))
    d_mlp = (layer_scale * grad_f).astype(jnp.bfloat16).reshape(rows * cols, chans)
    d_act = lax.dot_general(
        d_mlp, down_full, (((1,), (1,)), ((), ())), preferred_element_type=jnp.float32
    )
    d_pre = gelu_back(d_act)[0].astype(jnp.bfloat16)
    d_ln = lax.dot_general(
        d_pre, up_full, (((1,), (1,)), ((), ())), preferred_element_type=jnp.float32
    )
    d_ln = d_ln.reshape(rows, cols, chans)
    gain_term = jnp.sum(d_ln * normed, axis=(0, 1))
    d_norm = d_ln * ln_gain
    d_conv = rstd * (
        d_norm
        - jnp.mean(d_norm, axis=-1, keepdims=True)
        - normed * jnp.mean(d_norm * normed, axis=-1, keepdims=True)
    )
    kernel_rows = []
    for i in range(KW):
        kernel_cols = []
        for j in range(KW):
            kernel_cols.append(jnp.sum(d_conv * padded_x[i : i + rows, j : j + cols], axis=(0, 1)))
        kernel_rows.append(jnp.stack(kernel_cols))
    kernel_term = jnp.stack(kernel_rows)
    padded_grad = with_halo(d_conv[None].astype(jnp.bfloat16), (("sx", 1), ("sy", 2)), 3).astype(
        jnp.float32
    )[0]
    back_conv = grad_f
    for i in range(KW):
        for j in range(KW):
            back_conv = (
                back_conv
                + dw_kernel[i, j] * padded_grad[6 - i : 6 - i + rows, 6 - j : 6 - j + cols]
            )
    grad_input = back_conv.astype(jnp.bfloat16)
    grad_kernel, grad_gain, grad_scale = lax.psum(
        (kernel_term, gain_term, scale_term), ("sx", "sy", "fsdp")
    )
    return (block_out[None], grad_input[None], grad_kernel, grad_gain, grad_scale)


def solution(mesh):
    placed = (
        P("fsdp", "sx", "sy", None),
        P("fsdp", "sx", "sy", None),
        P(),
        P(),
        P(),
        P(),
        P("fsdp", None),
        P(),
        P(None, "fsdp"),
        P(),
        P(),
        P("fsdp", "sx", "sy", None),
    )
    return jax.shard_map(
        on_device,
        mesh=mesh,
        in_specs=placed,
        out_specs=(P("fsdp", "sx", "sy", None), P("fsdp", "sx", "sy", None), P(), P(), P()),
        check_vma=False,
    )
```

profile of v0, /device:TPU:1, one launch (start us, length us, event | category | flops | bytes accessed | tf_op | source)
XLA Modules:
  0.0 522.2 jit_solution(14191568544540321584)
XLA Ops:
  7.2 0.0 all-gather.3.cloned.1.call-start
  7.2 0.7 all-gather.3.cloned.1.call-update
  7.9 0.0 all-gather.5.cloned.1.call-start
  7.9 0.7 all-gather.5.cloned.1.call-update
  8.7 0.0 all-reduce.3.cloned.1.call-start
  8.7 0.9 exponential_bitcast_fusion
  9.6 0.1 copy.18
  9.7 0.3 mul.1066
  10.0 0.0 copy-start.5
  10.0 0.1 mul.1067
  10.2 0.1 multiply_convert_fusion.2
  10.3 4.5 collective-permute-start
  14.8 1.9 collective-permute-start.1
  16.8 0.3 slice_reduce_fusion.48
  17.2 0.9 slice_reduce_fusion.47
  18.3 3.0 collective-permute-done.1
  21.3 0.1 pad_maximum_fusion.3
  21.4 4.4 collective-permute-start.2
  25.8 1.3 collective-permute-start.3
  27.1 0.8 slice_reduce_fusion.46
  27.8 0.2 collective-permute-done.2
  28.1 5.4 %collective-permute-done.3 = bf16[1,14,3,1536]{3,2,1,0:T(4,128)(2,1)S(1)} collective-permute-done((bf16[1,14,3,1536]{3,2,1,0:T(4,128)(2,1)S(1)}, bf16[1,14,3,1536]{3,2,1,0:T(4,128)(2,1)S(1)}, u32[]{:S(2)}, u32[]{:S(2)}) %collective-permute-start.3) | collective-permute-done | bytes 129056 | tf_op jit(solution)/shard_map/ppermute | solution.py:18
  33.5 0.4 fusion.7
  34.2 0.0 copy-start.8
  34.2 9.4 %fusion.84 = (f32[8,16]{1,0:T(8,128)S(1)}, f32[8,16,1536]{2,1,0:T(8,128)S(1)}) fusion(f32[14,22,1536]{2,1,0:T(8,128)S(1)} %fusion.7, f32[1536]{0:T(1024)} %get-tuple-element.103, f32[1536]{0:T(1024)} %get-tuple-element.104, f32[1536]{0:T(1024)S(1)} %get-tuple-element.57, f32[1536]{0:T(1024)S(1)} %get-tuple-element.58, f32[1536]{0:T(1024)S(1)} %get-tuple-element.59, ...), kind=kLoop, calls=%fused_computation.267 | loop fusion | flops 19464064 | bytes 39629312 | tf_op jit(solution)/shard_map/reduce_sum | solution.py:55
  43.7 0.0 copy-start.50
  43.7 0.2 multiply_reduce_fusion.52
  43.9 1.7 add_convert_fusion.1
  45.6 71.9 %all-gather.3.cloned.1.call-done = bf16[1536,3072]{1,0:T(8,128)(2,1)} async-done(((bf16[48,3072]{1,0:T(8,128)(2,1)}), bf16[1536,3072]{1,0:T(8,128)(2,1)}) %all-gather.3.cloned.1.call-update) | async-done | bytes 9437200 | tf_op jit(solution)/shard_map/all_gather | solution.py:47
  117.5 6.4 %convolution_add_fusion = f32[128,3072]{1,0:T(8,128)} fusion(bf16[128,1536]{1,0:T(8,128)(2,1)} %bitcast.55, bf16[1536,3072]{1,0:T(8,128)(2,1)} %all-gather.3.cloned.1.call-done, f32[3072]{0:T(1024)S(1)} %copy-done.50), kind=kOutput, calls=%fused_computation | convolution fusion | flops 1208352768 | bytes 11415552 | tf_op jit(solution)/shard_map/dot_general | solution.py:60
  124.0 96.8 %all-gather.5.cloned.1.call-done = bf16[3072,1536]{0,1:T(8,128)(2,1)} async-done(((bf16[3072,48]{0,1:T(8,128)(2,1)}), bf16[3072,1536]{0,1:T(8,128)(2,1)}) %all-gather.5.cloned.1.call-update) | async-done | bytes 9437200 | tf_op jit(solution)/shard_map/all_gather | solution.py:48
  220.8 8.9 %fusion.61 = (f32[1536]{0:T(1024)}, bf16[128,1536]{1,0:T(8,128)(2,1)}, f32[128,1536]{1,0:T(8,128)}) fusion(bf16[1,8,16,1536]{3,2,1,0:T(8,128)(2,1)} %param.23, f32[1536]{0:T(1024)S(1)} %copy-done.51, f32[1536]{0:T(1024)S(1)} %copy-done.54, bf16[3072,1536]{0,1:T(8,128)(2,1)} %all-gather.5.cloned.1.call-done, f32[128,3072]{1,0:T(8,128)} %convolution_add_fusion), kind=kOutput, calls=%fused_computation.119 | convolution fusion | flops 1212676608 | bytes 12601344 | tf_op jit(solution)/shard_map/dot_general | solution.py:62
  229.7 13.3 %multiply_reduce_fusion.51 = (f32[128]{0:T(128)S(1)}, f32[128,1536]{1,0:T(8,128)}) fusion(f32[1536]{0:T(1024)S(1)} %copy-done.8, bf16[1536,3072]{1,0:T(8,128)(2,1)} %all-gather.3.cloned.1.call-done, f32[128,3072]{1,0:T(8,128)} %convolution_add_fusion, bf16[128,1536]{1,0:T(8,128)(2,1)} %get-tuple-element.118, ...), kind=kOutput, calls=%fused_computation.172 | convolution fusion | flops 2424176640 | bytes 21633536 | tf_op jit(solution)/shard_map/dot_general | solution.py:72
  243.0 0.1 div.17
  243.1 2.4 multiply_reduce_fusion
  245.5 2.6 multiply_reduce_fusion.1
  248.1 1.4 multiply_reduce_fusion.37
  249.6 2.0 multiply_reduce_fusion.19
  251.6 0.9 add_convert_fusion
  253.0 0.1 stack.199
  253.1 4.1 collective-permute-start.4
  257.2 1.9 collective-permute-start.5
  259.1 0.1 stack.208
  259.2 0.1 stack.217
  259.3 0.1 stack.226
  259.4 0.1 stack.235
  259.5 0.1 stack.244
  259.7 0.1 stack.253
  259.8 3.9 collective-permute-done.5
  263.7 0.1 fusion.83
  263.8 0.1 fusion.85
  263.9 4.3 collective-permute-start.6
  268.3 1.3 collective-permute-start.7
  269.6 0.0 copy-start.2
  269.6 0.7 copy-done.2
  270.3 0.0 all-reduce.3.cloned.1.call-update
  270.3 0.0 copy-start.3
  270.4 75.8 %all-reduce = (f32[1536]{0:T(1024)}, f32[1536]{0:T(1024)}) all-reduce(f32[1536]{0:T(1024)S(1)} %copy-done.49, f32[1536]{0:T(1024)S(1)} %copy-done.53), channel_id=1, replica_groups=mesh['sx'=4,'sy'=2,'fsdp'=32] {'sx','sy','fsdp'}, use_global_device_ids=true, to_apply=%region_55.0 | all-reduce | flops 3072 | bytes 24576 | tf_op jit(solution)/shard_map/psum | solution.py:101
  346.3 0.6 copy-done.6
  346.9 0.1 copy-done.7
  347.0 1.4 maximum_convert_fusion
  348.4 7.7 %fusion.72 = bf16[1,8,16,1536]{3,2,1,0:T(8,128)(2,1)} fusion(f32[14,22,1536]{2,1,0:T(8,128)S(1)} %maximum_convert_fusion, f32[1536]{0:T(1024)} %get-tuple-element.103, f32[1536]{0:T(1024)} %get-tuple-element.104, f32[1536]{0:T(1024)S(1)} %get-tuple-element.57, f32[1536]{0:T(1024)S(1)} %copy-done.10, f32[1536]{0:T(1024)S(1)} %copy-done.12, ...), kind=kLoop, calls=%fused_computation.191 | loop fusion | flops 19660800 | bytes 39622656 | tf_op jit(solution)/shard_map/broadcast_in_dim | solution.py:104
  356.1 157.8 %all-reduce.3.cloned.1.call-done = f32[7,7,1536]{2,1,0:T(8,128)} async-done(((f32[7,7,1536]{2,1,0:T(8,128)}), f32[7,7,1536]{2,1,0:T(8,128)}) %all-reduce.3.cloned.1.call-update) | async-done | bytes 301072 | tf_op jit(solution)/shard_map/psum | solution.py:101
  514.0 1.7 copy.26
  (168 shorter events, 0.6 us)
Async XLA Ops:
  7.2 110.4 %all-gather.3.cloned.1.call-start = ((), (), s32[]{:S(2)}) async-start(), calls=%async_computation | async-start | bytes 9732096 | tf_op jit(solution)/shard_map/all_gather | solution.py:47
  7.9 212.9 %all-gather.5.cloned.1.call-start = ((), (), s32[]{:S(2)}) async-start(), calls=%async_computation.1 | async-start | bytes 9732096 | tf_op jit(solution)/shard_map/all_gather | solution.py:48
  8.6 1.5 copy-start.4
  8.7 505.3 %all-reduce.3.cloned.1.call-start = ((), (), s32[]{:S(2)}) async-start(), calls=%async_computation.2 | async-start | bytes 688128 | tf_op jit(solution)/shard_map/psum | solution.py:101
  10.0 6.7 %copy-start.5 = (f32[7,7,1536]{2,1,0:T(8,128)S(1)}, f32[7,7,1536]{2,1,0:T(8,128)}, u32[]{:S(2)}) copy-start(f32[7,7,1536]{2,1,0:T(8,128)} %param.14) | copy-start | bytes 903172
  10.3 8.0 %collective-permute-start = (bf16[1,3,16,1536]{3,2,1,0:T(8,128)(2,1)S(1)}, bf16[1,3,16,1536]{3,2,1,0:T(8,128)(2,1)S(1)}, u32[]{:S(2)}, u32[]{:S(2)}) collective-permute-start(bf16[1,3,16,1536]{3,2,1,0:T(8,128)(2,1)S(1)} %get-tuple-element.121), channel_id=1, source_target_pairs={{0,64},{64,128},{128,192},{1,65},{65,129},{129,193},{2,66},{66,130... | collective-permute-start | bytes 442376 | tf_op jit(solution)/shard_map/ppermute | solution.py:17
  14.8 6.5 %collective-permute-start.1 = (bf16[1,3,16,1536]{3,2,1,0:T(8,128)(2,1)S(1)}, bf16[1,3,16,1536]{3,2,1,0:T(8,128)(2,1)S(1)}, u32[]{:S(2)}, u32[]{:S(2)}) collective-permute-start(bf16[1,3,16,1536]{3,2,1,0:T(8,128)(2,1)S(1)} %get-tuple-element.122), channel_id=1, source_target_pairs={{64,0},{128,64},{192,128},{65,1},{129,65},{193,129},{66,2},{130,66... | collective-permute-start | bytes 442376 | tf_op jit(solution)/shard_map/ppermute | solution.py:18
  17.1 16.8 %copy-start.9 = (f32[1536]{0:T(1024)}, f32[1536]{0:T(1024)S(1)}, u32[]{:S(2)}) copy-start(f32[1536]{0:T(1024)S(1)} %get-tuple-element.58) | copy-start | bytes 18436
  17.1 16.8 %copy-start.11 = (f32[1536]{0:T(1024)}, f32[1536]{0:T(1024)S(1)}, u32[]{:S(2)}) copy-start(f32[1536]{0:T(1024)S(1)} %get-tuple-element.59) | copy-start | bytes 18436
  17.1 16.8 %copy-start.13 = (f32[1536]{0:T(1024)}, f32[1536]{0:T(1024)S(1)}, u32[]{:S(2)}) copy-start(f32[1536]{0:T(1024)S(1)} %get-tuple-element.60) | copy-start | bytes 18436
  17.1 16.8 %copy-start.15 = (f32[1536]{0:T(1024)}, f32[1536]{0:T(1024)S(1)}, u32[]{:S(2)}) copy-start(f32[1536]{0:T(1024)S(1)} %get-tuple-element.61) | copy-start | bytes 18436
  17.1 16.8 %copy-start.17 = (f32[1536]{0:T(1024)}, f32[1536]{0:T(1024)S(1)}, u32[]{:S(2)}) copy-start(f32[1536]{0:T(1024)S(1)} %get-tuple-element.62) | copy-start | bytes 18436
  17.1 16.8 %copy-start.19 = (f32[1536]{0:T(1024)}, f32[1536]{0:T(1024)S(1)}, u32[]{:S(2)}) copy-start(f32[1536]{0:T(1024)S(1)} %get-tuple-element.63) | copy-start | bytes 18436
  17.1 16.8 %copy-start.21 = (f32[1536]{0:T(1024)}, f32[1536]{0:T(1024)S(1)}, u32[]{:S(2)}) copy-start(f32[1536]{0:T(1024)S(1)} %get-tuple-element.64) | copy-start | bytes 18436
  17.1 16.8 %copy-start.22 = (f32[1536]{0:T(1024)}, f32[1536]{0:T(1024)S(1)}, u32[]{:S(2)}) copy-start(f32[1536]{0:T(1024)S(1)} %get-tuple-element.65) | copy-start | bytes 18436
  17.2 16.8 %copy-start.23 = (f32[1536]{0:T(1024)}, f32[1536]{0:T(1024)S(1)}, u32[]{:S(2)}) copy-start(f32[1536]{0:T(1024)S(1)} %get-tuple-element.66) | copy-start | bytes 18436
  17.2 16.8 %copy-start.24 = (f32[1536]{0:T(1024)}, f32[1536]{0:T(1024)S(1)}, u32[]{:S(2)}) copy-start(f32[1536]{0:T(1024)S(1)} %get-tuple-element.67) | copy-start | bytes 18436
  17.2 16.8 %copy-start.25 = (f32[1536]{0:T(1024)}, f32[1536]{0:T(1024)S(1)}, u32[]{:S(2)}) copy-start(f32[1536]{0:T(1024)S(1)} %get-tuple-element.68) | copy-start | bytes 18436
  17.2 16.8 %copy-start.26 = (f32[1536]{0:T(1024)}, f32[1536]{0:T(1024)S(1)}, u32[]{:S(2)}) copy-start(f32[1536]{0:T(1024)S(1)} %get-tuple-element.69) | copy-start | bytes 18436
  17.2 16.8 %copy-start.27 = (f32[1536]{0:T(1024)}, f32[1536]{0:T(1024)S(1)}, u32[]{:S(2)}) copy-start(f32[1536]{0:T(1024)S(1)} %get-tuple-element.70) | copy-start | bytes 18436
  17.2 16.8 %copy-start.28 = (f32[1536]{0:T(1024)}, f32[1536]{0:T(1024)S(1)}, u32[]{:S(2)}) copy-start(f32[1536]{0:T(1024)S(1)} %get-tuple-element.71) | copy-start | bytes 18436
  17.2 16.8 %copy-start.29 = (f32[1536]{0:T(1024)}, f32[1536]{0:T(1024)S(1)}, u32[]{:S(2)}) copy-start(f32[1536]{0:T(1024)S(1)} %get-tuple-element.72) | copy-start | bytes 18436
  17.2 16.8 %copy-start.30 = (f32[1536]{0:T(1024)}, f32[1536]{0:T(1024)S(1)}, u32[]{:S(2)}) copy-start(f32[1536]{0:T(1024)S(1)} %get-tuple-element.73) | copy-start | bytes 18436
  17.2 16.8 %copy-start.31 = (f32[1536]{0:T(1024)}, f32[1536]{0:T(1024)S(1)}, u32[]{:S(2)}) copy-start(f32[1536]{0:T(1024)S(1)} %get-tuple-element.74) | copy-start | bytes 18436
  18.2 15.9 %copy-start.32 = (f32[1536]{0:T(1024)}, f32[1536]{0:T(1024)S(1)}, u32[]{:S(2)}) copy-start(f32[1536]{0:T(1024)S(1)} %get-tuple-element.75) | copy-start | bytes 18436
  18.2 15.9 %copy-start.33 = (f32[1536]{0:T(1024)}, f32[1536]{0:T(1024)S(1)}, u32[]{:S(2)}) copy-start(f32[1536]{0:T(1024)S(1)} %get-tuple-element.76) | copy-start | bytes 18436
  18.2 15.9 %copy-start.34 = (f32[1536]{0:T(1024)}, f32[1536]{0:T(1024)S(1)}, u32[]{:S(2)}) copy-start(f32[1536]{0:T(1024)S(1)} %get-tuple-element.77) | copy-start | bytes 18436
  18.2 15.9 %copy-start.35 = (f32[1536]{0:T(1024)}, f32[1536]{0:T(1024)S(1)}, u32[]{:S(2)}) copy-start(f32[1536]{0:T(1024)S(1)} %get-tuple-element.78) | copy-start | bytes 18436
  18.2 15.9 %copy-start.36 = (f32[1536]{0:T(1024)}, f32[1536]{0:T(1024)S(1)}, u32[]{:S(2)}) copy-start(f32[1536]{0:T(1024)S(1)} %get-tuple-element.79) | copy-start | bytes 18436
  18.2 15.9 %copy-start.37 = (f32[1536]{0:T(1024)}, f32[1536]{0:T(1024)S(1)}, u32[]{:S(2)}) copy-start(f32[1536]{0:T(1024)S(1)} %get-tuple-element.80) | copy-start | bytes 18436
  18.2 15.9 %copy-start.38 = (f32[1536]{0:T(1024)}, f32[1536]{0:T(1024)S(1)}, u32[]{:S(2)}) copy-start(f32[1536]{0:T(1024)S(1)} %get-tuple-element.81) | copy-start | bytes 18436
  18.2 15.9 %copy-start.39 = (f32[1536]{0:T(1024)}, f32[1536]{0:T(1024)S(1)}, u32[]{:S(2)}) copy-start(f32[1536]{0:T(1024)S(1)} %get-tuple-element.82) | copy-start | bytes 18436
  18.2 15.9 %copy-start.40 = (f32[1536]{0:T(1024)}, f32[1536]{0:T(1024)S(1)}, u32[]{:S(2)}) copy-start(f32[1536]{0:T(1024)S(1)} %get-tuple-element.83) | copy-start | bytes 18436
  18.2 15.9 %copy-start.41 = (f32[1536]{0:T(1024)}, f32[1536]{0:T(1024)S(1)}, u32[]{:S(2)}) copy-start(f32[1536]{0:T(1024)S(1)} %get-tuple-element.84) | copy-start | bytes 18436
  18.2 15.9 %copy-start.42 = (f32[1536]{0:T(1024)}, f32[1536]{0:T(1024)S(1)}, u32[]{:S(2)}) copy-start(f32[1536]{0:T(1024)S(1)} %get-tuple-element.85) | copy-start | bytes 18436
  18.2 15.9 %copy-start.43 = (f32[1536]{0:T(1024)}, f32[1536]{0:T(1024)S(1)}, u32[]{:S(2)}) copy-start(f32[1536]{0:T(1024)S(1)} %get-tuple-element.86) | copy-start | bytes 18436
  18.2 15.9 %copy-start.44 = (f32[1536]{0:T(1024)}, f32[1536]{0:T(1024)S(1)}, u32[]{:S(2)}) copy-start(f32[1536]{0:T(1024)S(1)} %get-tuple-element.87) | copy-start | bytes 18436
  18.3 15.9 %copy-start.45 = (f32[1536]{0:T(1024)}, f32[1536]{0:T(1024)S(1)}, u32[]{:S(2)}) copy-start(f32[1536]{0:T(1024)S(1)} %get-tuple-element.88) | copy-start | bytes 18436
  18.3 15.9 %copy-start.46 = (f32[1536]{0:T(1024)}, f32[1536]{0:T(1024)S(1)}, u32[]{:S(2)}) copy-start(f32[1536]{0:T(1024)S(1)} %get-tuple-element.89) | copy-start | bytes 18436
  18.3 15.9 %copy-start.47 = (f32[1536]{0:T(1024)}, f32[1536]{0:T(1024)S(1)}, u32[]{:S(2)}) copy-start(f32[1536]{0:T(1024)S(1)} %get-tuple-element.90) | copy-start | bytes 18436
  18.3 15.9 %copy-start.48 = (f32[1536]{0:T(1024)}, f32[1536]{0:T(1024)S(1)}, u32[]{:S(2)}) copy-start(f32[1536]{0:T(1024)S(1)} %get-tuple-element.91) | copy-start | bytes 18436
  21.4 6.7 %collective-permute-start.2 = (bf16[1,14,3,1536]{3,2,1,0:T(4,128)(2,1)S(1)}, bf16[1,14,3,1536]{3,2,1,0:T(4,128)(2,1)S(1)}, u32[]{:S(2)}, u32[]{:S(2)}) collective-permute-start(bf16[1,14,3,1536]{3,2,1,0:T(4,128)(2,1)S(1)} %get-tuple-element.115), channel_id=1, source_target_pairs={{0,32},{1,33},{2,34},{3,35},{4,36},{5,37},{6,38},{7,39},{8,40},{9,... | collective-permute-start | bytes 387080 | tf_op jit(solution)/shard_map/ppermute | solution.py:17
  25.8 7.7 %collective-permute-start.3 = (bf16[1,14,3,1536]{3,2,1,0:T(4,128)(2,1)S(1)}, bf16[1,14,3,1536]{3,2,1,0:T(4,128)(2,1)S(1)}, u32[]{:S(2)}, u32[]{:S(2)}) collective-permute-start(bf16[1,14,3,1536]{3,2,1,0:T(4,128)(2,1)S(1)} %get-tuple-element.116), channel_id=1, source_target_pairs={{32,0},{33,1},{34,2},{35,3},{36,4},{37,5},{38,6},{39,7},{40,8},{41... | collective-permute-start | bytes 387080 | tf_op jit(solution)/shard_map/ppermute | solution.py:18
  34.2 9.7 %copy-start.8 = (f32[1536]{0:T(1024)S(1)}, f32[1536]{0:T(1024)}, u32[]{:S(2)}) copy-start(f32[1536]{0:T(1024)} %param.16) | copy-start | bytes 18436
  43.7 73.9 %copy-start.50 = (f32[3072]{0:T(1024)S(1)}, f32[3072]{0:T(1024)}, u32[]{:S(2)}) copy-start(f32[3072]{0:T(1024)} %param.19) | copy-start | bytes 36868
  117.5 103.2 %copy-start.51 = (f32[1536]{0:T(1024)S(1)}, f32[1536]{0:T(1024)}, u32[]{:S(2)}) copy-start(f32[1536]{0:T(1024)} %param.22) | copy-start | bytes 18436
  117.5 103.2 %copy-start.54 = (f32[1536]{0:T(1024)S(1)}, f32[1536]{0:T(1024)}, u32[]{:S(2)}) copy-start(f32[1536]{0:T(1024)} %param.21) | copy-start | bytes 18436
  243.1 2.4 copy-start
  249.6 2.0 copy-start.1
  249.6 2.0 copy-start.52
  253.1 6.7 %collective-permute-start.4 = (bf16[1,3,16,1536]{3,2,1,0:T(8,128)(2,1)S(1)}, bf16[1,3,16,1536]{3,2,1,0:T(8,128)(2,1)S(1)}, u32[]{:S(2)}, u32[]{:S(2)}) collective-permute-start(bf16[1,3,16,1536]{3,2,1,0:T(8,128)(2,1)S(1)} %get-tuple-element.119), channel_id=1, source_target_pairs={{0,64},{64,128},{128,192},{1,65},{65,129},{129,193},{2,66},{66,130... | collective-permute-start | bytes 442376 | tf_op jit(solution)/shard_map/ppermute | solution.py:17
  257.2 6.5 %collective-permute-start.5 = (bf16[1,3,16,1536]{3,2,1,0:T(8,128)(2,1)S(1)}, bf16[1,3,16,1536]{3,2,1,0:T(8,128)(2,1)S(1)}, u32[]{:S(2)}, u32[]{:S(2)}) collective-permute-start(bf16[1,3,16,1536]{3,2,1,0:T(8,128)(2,1)S(1)} %get-tuple-element.120), channel_id=1, source_target_pairs={{64,0},{128,64},{192,128},{65,1},{129,65},{193,129},{66,2},{130,66... | collective-permute-start | bytes 442376 | tf_op jit(solution)/shard_map/ppermute | solution.py:18
  259.8 10.6 %copy-start.49 = (f32[1536]{0:T(1024)S(1)}, f32[1536]{0:T(1024)}, u32[]{:S(2)}) copy-start(f32[1536]{0:T(1024)} %get-tuple-element.54) | copy-start | bytes 18436
  259.8 10.6 %copy-start.53 = (f32[1536]{0:T(1024)S(1)}, f32[1536]{0:T(1024)}, u32[]{:S(2)}) copy-start(f32[1536]{0:T(1024)} %get-tuple-element.117) | copy-start | bytes 18436
  263.9 82.3 %collective-permute-start.6 = (bf16[1,14,3,1536]{3,2,1,0:T(4,128)(2,1)S(1)}, bf16[1,14,3,1536]{3,2,1,0:T(4,128)(2,1)S(1)}, u32[]{:S(2)}, u32[]{:S(2)}) collective-permute-start(bf16[1,14,3,1536]{3,2,1,0:T(4,128)(2,1)S(1)} %get-tuple-element.111), channel_id=1, source_target_pairs={{0,32},{1,33},{2,34},{3,35},{4,36},{5,37},{6,38},{7,39},{8,40},{9,... | collective-permute-start | bytes 387080 | tf_op jit(solution)/shard_map/ppermute | solution.py:17
  268.3 78.0 %collective-permute-start.7 = (bf16[1,14,3,1536]{3,2,1,0:T(4,128)(2,1)S(1)}, bf16[1,14,3,1536]{3,2,1,0:T(4,128)(2,1)S(1)}, u32[]{:S(2)}, u32[]{:S(2)}) collective-permute-start(bf16[1,14,3,1536]{3,2,1,0:T(4,128)(2,1)S(1)} %get-tuple-element.112), channel_id=1, source_target_pairs={{32,0},{33,1},{34,2},{35,3},{36,4},{37,5},{38,6},{39,7},{40,8},{41... | collective-permute-start | bytes 387080 | tf_op jit(solution)/shard_map/ppermute | solution.py:18
  269.6 0.7 copy-start.2
  270.3 78.0 %copy-start.3 = (bf16[1,8,16,1536]{3,2,1,0:T(8,128)(2,1)S(1)}, bf16[1,8,16,1536]{3,2,1,0:T(8,128)(2,1)}, u32[]{:S(2)}) copy-start(bf16[1,8,16,1536]{3,2,1,0:T(8,128)(2,1)} %param.23) | copy-start | bytes 1179652
  270.3 78.0 %copy-start.10 = (f32[1536]{0:T(1024)S(1)}, f32[1536]{0:T(1024)}, u32[]{:S(2)}) copy-start(f32[1536]{0:T(1024)} %copy-done.9) | copy-start | bytes 18436
  270.3 78.0 %copy-start.12 = (f32[1536]{0:T(1024)S(1)}, f32[1536]{0:T(1024)}, u32[]{:S(2)}) copy-start(f32[1536]{0:T(1024)} %copy-done.11) | copy-start | bytes 18436
  270.4 78.0 %copy-start.14 = (f32[1536]{0:T(1024)S(1)}, f32[1536]{0:T(1024)}, u32[]{:S(2)}) copy-start(f32[1536]{0:T(1024)} %copy-done.13) | copy-start | bytes 18436
  270.4 78.0 %copy-start.16 = (f32[1536]{0:T(1024)S(1)}, f32[1536]{0:T(1024)}, u32[]{:S(2)}) copy-start(f32[1536]{0:T(1024)} %copy-done.15) | copy-start | bytes 18436
  270.4 78.0 %copy-start.18 = (f32[1536]{0:T(1024)S(1)}, f32[1536]{0:T(1024)}, u32[]{:S(2)}) copy-start(f32[1536]{0:T(1024)} %copy-done.17) | copy-start | bytes 18436
  270.4 78.0 %copy-start.20 = (f32[1536]{0:T(1024)S(1)}, f32[1536]{0:T(1024)}, u32[]{:S(2)}) copy-start(f32[1536]{0:T(1024)} %copy-done.19) | copy-start | bytes 18436
  (2 other events, 1.4 us)
Sparse Core Ops, SparseCore 0:
  10.6 106.9 all-gather.2
  120.1 100.5 all-gather.4
  270.4 243.4 all-reduce.2
where the time goes:
time: 523 us; the launch traced here: 522 us
  waiting for transfers between devices  340 us (65%)
  blocking collectives  75.8 us (14%)
  other arithmetic  31.2 us (6%)
  matrix products  28.6 us (5%)
  starting transfers between devices  23.8 us (5%)
  between operations  15.1 us (3%)
  local copies, waits for them, and re-layouts  7.13 us (1%)
    psum x1, waiting for transfers between devices, on_device(): lax.psum((kernel_term, gain_term, scale_term), ('sx', 'sy', 'fsdp'))  158 us
    all_gather x1, waiting for transfers between devices, on_device(): lax.all_gather(w_down, 'fsdp', axis=1, tiled=True)  96.8 us
    psum x1, blocking collectives, on_device(): lax.psum((kernel_term, gain_term, scale_term), ('sx', 'sy', 'fsdp'))  75.8 us
    all_gather x1, waiting for transfers between devices, on_device(): lax.all_gather(w_up, 'fsdp', axis=0, tiled=True)  71.9 us
    ppermute x4, starting transfers between devices, with_halo(): before = lax.ppermute(last, axis, up)  17.3 us
    dot_general x1, matrix products, on_device(): lax.dot_general(d_pre, up_full, (((1,), (1,)), ((), ())), preferred_eleme...  13.3 us
    ppermute x4, waiting for transfers between devices, with_halo(): after = lax.ppermute(initial, axis, down)  12.2 us
  transfers between devices with their start and end apart: 11, of which 7 were waited for; matrix products, arithmetic and copies ran while one was open for 6% of the time, Pallas kernels for 0%

commit v1 on v0

--- a/solution.py
+++ b/solution.py
@@ -1,10 +1,284 @@
+import functools
+
 import jax
 import jax.numpy as jnp
 from jax import lax
+from jax.experimental import pallas as pl
+from jax.experimental.pallas import tpu as pltpu
 from jax.sharding import PartitionSpec as P
 
 CG = 128
 KW = 7
+NB = 12
+ROWS, COLS, CHANS = 8, 16, 1536
+PR, PC = 16, 32
+PIECE = 11
+MESH = pl.DeviceIdType.MESH
+
+
+def remote(src, dst, send, recv, where):
+    return pltpu.make_async_remote_copy(
+        src_ref=src, dst_ref=dst, send_sem=send, recv_sem=recv, device_id=where, device_id_type=MESH
+    )
+
+
+def row_halo(buf, send, recv, sx, act):
+    down = remote(buf.at[:, 8:11, 8:24, :], buf.at[:, 0:3, 8:24, :], send.at[0], recv.at[0], {"sx": sx + 1})
+    up = remote(buf.at[:, 3:6, 8:24, :], buf.at[:, 11:14, 8:24, :], send.at[1], recv.at[1], {"sx": sx - 1})
+    if act == "start":
+
+        @pl.when(sx < 3)
+        def _():
+            down.start()
+
+        @pl.when(sx > 0)
+        def _():
+            up.start()
+
+    else:
+
+        @pl.when(sx < 3)
+        def _():
+            up.wait_recv()
+            down.wait_send()
+
+        @pl.when(sx > 0)
+        def _():
+            down.wait_recv()
+            up.wait_send()
+
+
+def zero_rows(buf, sx):
+    @pl.when(sx == 0)
+    def _():
+        buf[:, 0:3, :, :] = jnp.zeros((NB, 3, PC, 128), jnp.float32)
+
+    @pl.when(sx == 3)
+    def _():
+        buf[:, 11:14, :, :] = jnp.zeros((NB, 3, PC, 128), jnp.float32)
+
+
+def pack_cols(buf, stage, sy):
+    for side, first in ((0, 21), (1, 8)):
+
+        @pl.when(sy == side)
+        def _():
+            @pl.loop(0, NB)
+            def _(b):
+                for c in range(3):
+                    at = pl.multiple_of(b * 16, 16)
+                    stage[c, pl.ds(at, 16), :] = buf[b, :, first + c, :].astype(jnp.bfloat16)
+
+
+def unpack_cols(buf, stage, sy):
+    for side, first, other in ((0, 24, 5), (1, 5, 24)):
+
+        @pl.when(sy == side)
+        def _():
+            @pl.loop(0, NB)
+            def _(b):
+                for c in range(3):
+                    at = pl.multiple_of(b * 16, 16)
+                    buf[b, :, first + c, :] = stage[c, pl.ds(at, 16), :].astype(jnp.float32)
+                    buf[b, :, other + c, :] = jnp.zeros((PR, 128), jnp.float32)
+
+
+def lanes(b):
+    return pl.ds(pl.multiple_of(b * 128, 128), 128)
+
+
+def depthwise(buf, b, taps, start, flip):
+    acc = start
+    for j in range(KW):
+        jj = 6 - j if flip else j
+        shifted = buf[b, 0:14, 5 + jj : 21 + jj, :]
+        for i in range(KW):
+            ii = 6 - i if flip else i
+            acc = acc + taps[i, j, lanes(b)].reshape(1, 1, 128) * shifted[ii : ii + ROWS]
+    return acc
+
+
+def kernel_grad(xbuf, gbuf, grads, b):
+    g = gbuf[b, 3:11, 8:24, :]
+    for j in range(KW):
+        shifted = xbuf[b, 0:14, 5 + j : 21 + j, :]
+        for i in range(KW):
+            q = jnp.sum(g * shifted[i : i + ROWS], axis=0)
+            grads[b * 7 + i, j, :] = jnp.sum(q, axis=0)
+
+
+def tail_kernel(
+    xp, dc, cot, taps, extra, gi, gk, gg, gs,
+    gp, stage, landed, grads, got1, part, got2, fin, full,
+    hs, hr, cs, cr, s1, r1, s2, r2, s3, r3, s4, r4,
+):
+    sx, sy, f = lax.axis_index("sx"), lax.axis_index("sy"), lax.axis_index("fsdp")
+    g = sx * 2 + sy
+
+    def peer(k):
+        p = lax.rem(g + k, 8)
+        return p, {"sx": p // 2, "sy": lax.rem(p, 2)}
+
+    barrier = pltpu.get_barrier_semaphore()
+    for k in range(1, 8):
+        pl.semaphore_signal(barrier, inc=1, device_id=peer(k)[1], device_id_type=MESH)
+
+    @pl.loop(1, 32)
+    def _(k):
+        pl.semaphore_signal(barrier, inc=1, device_id={"fsdp": lax.rem(f + k, 32)}, device_id_type=MESH)
+
+    gp[:, 3:11, 8:24, :] = dc[...]
+    zero_rows(gp, sx)
+    grads[84:88] = jnp.zeros((4, 8, 128), jnp.float32)
+    pl.semaphore_wait(barrier, 38)
+
+    row_halo(gp, hs, hr, sx, "start")
+
+    @pl.loop(0, 6)
+    def _(b):
+        kernel_grad(xp, gp, grads, b)
+
+    row_halo(gp, hs, hr, sx, "wait")
+    pack_cols(gp, stage, sy)
+    col = remote(stage, landed, cs, cr, {"sy": 1 - sy})
+    col.start()
+
+    @pl.loop(6, NB)
+    def _(b):
+        kernel_grad(xp, gp, grads, b)
+
+    for b in range(NB):
+        grads[b * 7, 7, :] = extra[0, b * 128 : (b + 1) * 128]
+        grads[b * 7 + 1, 7, :] = extra[1, b * 128 : (b + 1) * 128]
+        for i in range(2, 7):
+            grads[b * 7 + i, 7, :] = jnp.zeros((128,), jnp.float32)
+
+    first = []
+    for k in range(1, 8):
+        p, where = peer(k)
+        first.append(remote(grads.at[pl.ds(p * PIECE, PIECE)], got1.at[k - 1], s1.at[k - 1], r1.at[k - 1], where))
+        first[-1].start()
+
+    col.wait()
+    unpack_cols(gp, landed, sy)
+
+    def out_conv(b):
+        gi[:, :, lanes(b)] = depthwise(
+            gp, b, taps, cot[:, :, lanes(b)].astype(jnp.float32), True
+        ).astype(jnp.bfloat16)
+
+    pl.loop(0, 4)(out_conv)
+
+    total = grads[pl.ds(g * PIECE, PIECE)]
+    for k in range(7):
+        first[k].wait_recv()
+        total = total + got1[k]
+    part[...] = total
+
+    def to_owner(t):
+        owner = t * 3
+        slot = lax.rem(f - owner + 32, 32)
+        return remote(part.at[t], got2.at[slot], s2.at[t], r2.at[slot], {"fsdp": owner})
+
+    for t in range(PIECE):
+
+        @pl.when(f != t * 3)
+        def _():
+            to_owner(t).start()
+
+    pl.loop(4, 8)(out_conv)
+
+    mine = f // 3
+    owns = lax.rem(f, 3) == 0
+
+    def spread(k):
+        return remote(fin.at[mine], fin.at[mine], s3.at[k], r3.at[mine], {"fsdp": lax.rem(f + k, 32)})
+
+    @pl.when(owns)
+    def _():
+        fin[mine] = part[mine]
+
+        @pl.loop(1, 32)
+        def _(k):
+            remote(part.at[0], got2.at[k], s2.at[0], r2.at[k], {"fsdp": f}).wait_recv()
+            fin[mine] = fin[mine] + got2[k]
+
+        @pl.loop(1, 32)
+        def _(k):
+            spread(k).start()
+
+    pl.loop(8, NB)(out_conv)
+
+    for t in range(PIECE):
+
+        @pl.when(f != t * 3)
+        def _():
+            remote(fin.at[t], fin.at[t], s3.at[0], r3.at[t], {"fsdp": t * 3}).wait_recv()
+
+    last = []
+    for k in range(1, 8):
+        p, where = peer(k)
+        last.append(remote(fin, full.at[pl.ds(g * PIECE, PIECE)], s4.at[k - 1], r4.at[k - 1], where))
+        last[-1].start()
+    full[pl.ds(g * PIECE, PIECE)] = fin[...]
+    for k in range(7):
+        last[k].wait_recv()
+    for b in range(NB):
+        at = slice(b * 128, (b + 1) * 128)
+        for i in range(KW):
+            gk[i, :, at] = full[b * 7 + i, 0:7, :]
+        gg[0, at] = full[b * 7, 7, :]
+        gs[0, at] = full[b * 7 + 1, 7, :]
+
+    for k in range(7):
+        first[k].wait_send()
+        last[k].wait_send()
+    for t in range(PIECE):
+
+        @pl.when(f != t * 3)
+        def _():
+            to_owner(t).wait_send()
+
+    @pl.when(owns)
+    def _():
+        @pl.loop(1, 32)
+        def _(k):
+            spread(k).wait_send()
+
+
+def tail(xp, dc, cot, taps, extra):
+    vmem = pl.BlockSpec(memory_space=pltpu.VMEM)
+    dma = pltpu.SemaphoreType.DMA
+    f32, bf16 = jnp.float32, jnp.bfloat16
+    return pl.pallas_call(
+        tail_kernel,
+        out_shape=(
+            jax.ShapeDtypeStruct((ROWS, COLS, CHANS), bf16),
+            jax.ShapeDtypeStruct((KW, KW, CHANS), f32),
+            jax.ShapeDtypeStruct((1, CHANS), f32),
+            jax.ShapeDtypeStruct((1, CHANS), f32),
+        ),
+        in_specs=[vmem] * 5,
+        out_specs=(vmem,) * 4,
+        scratch_shapes=[
+            pltpu.VMEM((NB, PR, PC, 128), f32),
+            pltpu.VMEM((3, NB * 16, 128), bf16),
+            pltpu.VMEM((3, NB * 16, 128), bf16),
+            pltpu.VMEM((88, 8, 128), f32),
+            pltpu.VMEM((7, PIECE, 8, 128), f32),
+            pltpu.VMEM((PIECE, 8, 128), f32),
+            pltpu.VMEM((32, 8, 128), f32),
+            pltpu.VMEM((PIECE, 8, 128), f32),
+            pltpu.VMEM((88, 8, 128), f32),
+            dma((2,)), dma((2,)), dma, dma,
+            dma((7,)), dma((7,)), dma((PIECE,)), dma((32,)),
+            dma((32,)), dma((PIECE,)), dma((7,)), dma((7,)),
+        ],
+        compiler_params=pltpu.CompilerParams(
+            collective_id=1, has_side_effects=True, vmem_limit_bytes=40 * 2**20
+        ),
+        name="tail",
+    )(xp, dc, cot, taps, extra)
 
 
 def with_halo(shard, sides, width):
@@ -80,28 +354,13 @@
         - jnp.mean(d_norm, axis=-1, keepdims=True)
         - normed * jnp.mean(d_norm * normed, axis=-1, keepdims=True)
     )
-    kernel_rows = []
-    for i in range(KW):
-        kernel_cols = []
-        for j in range(KW):
-            kernel_cols.append(jnp.sum(d_conv * padded_x[i : i + rows, j : j + cols], axis=(0, 1)))
-        kernel_rows.append(jnp.stack(kernel_cols))
-    kernel_term = jnp.stack(kernel_rows)
-    padded_grad = with_halo(d_conv[None].astype(jnp.bfloat16), (("sx", 1), ("sy", 2)), 3).astype(
-        jnp.float32
-    )[0]
-    back_conv = grad_f
-    for i in range(KW):
-        for j in range(KW):
-            back_conv = (
-                back_conv
-                + dw_kernel[i, j] * padded_grad[6 - i : 6 - i + rows, 6 - j : 6 - j + cols]
-            )
-    grad_input = back_conv.astype(jnp.bfloat16)
-    grad_kernel, grad_gain, grad_scale = lax.psum(
-        (kernel_term, gain_term, scale_term), ("sx", "sy", "fsdp")
-    )
-    return (block_out[None], grad_input[None], grad_kernel, grad_gain, grad_scale)
+    blocked_x = padded_x.reshape(rows + 6, cols + 6, NB, 128).transpose(2, 0, 1, 3)
+    blocked_x = jnp.pad(blocked_x, ((0, 0), (0, 2), (5, 5), (0, 0)))
+    blocked_g = d_conv.reshape(rows, cols, NB, 128).transpose(2, 0, 1, 3)
+    grad_input, grad_kernel, grad_gain, grad_scale = tail(
+        blocked_x, blocked_g, cotangent[0], dw_kernel, jnp.stack([gain_term, scale_term])
+    )
+    return (block_out[None], grad_input[None], grad_kernel, grad_gain[0], grad_scale[0])
 
 
 def solution(mesh):

time: 523 us -> 297 us (0.57)
  waiting for transfers between devices: 340 us -> 172 us
  blocking collectives: 75.8 us -> 0 us
  Pallas kernels: 0 us -> 37.4 us
  starting transfers between devices: 23.8 us -> 12.2 us
  other arithmetic: 31.2 us -> 22.2 us
    psum x1 -> x0, waiting for transfers between devices: 158 us -> none  [on_device(): lax.psum((kernel_term, gain_term, scale_term), ('sx', 'sy', 'fsdp'))]
    psum x1 -> x0, blocking collectives: 75.8 us -> none  [on_device(): lax.psum((kernel_term, gain_term, scale_term), ('sx', 'sy', 'fsdp'))]
    pallas_call x0 -> x1, Pallas kernels: none -> 37.4 us  [tail(): pl.pallas_call(tail_kernel, out_shape=(jax.ShapeDtypeStruct((ROWS, COLS,...]
    ppermute x4 -> x2, starting transfers between devices: 17.3 us -> 8.87 us  [with_halo(): before = lax.ppermute(last, axis, up)]
    broadcast_in_dim x1 -> x0, other arithmetic: 7.69 us -> none  [on_device(): grad_input[None]]
    all_gather x1, waiting for transfers between devices: 71.9 us -> 65.1 us  [on_device(): lax.all_gather(w_up, 'fsdp', axis=0, tiled=True)]
    reduce_sum x3 -> x0, other arithmetic: 6.02 us -> none  [on_device(): jnp.sum(d_conv * padded_x[i:i + rows, j:j + cols], axis=(0, 1))]
    ppermute x4 -> x2, waiting for transfers between devices: 12.2 us -> 8.07 us  [with_halo(): after = lax.ppermute(initial, axis, down)]
  transfers between devices with their start and end apart: 11 -> 6, of which waited for: 7 -> 5; matrix products, arithmetic and copies ran while one was open for 6% -> 10% of each run, Pallas kernels for 0% -> 0%
where the time goes in v1:
time: 297 us
  waiting for transfers between devices  172 us (58%)
  Pallas kernels  37.4 us (13%)
  matrix products  27.6 us (9%)
  other arithmetic  22.2 us (7%)
  between operations  14.8 us (5%)
  starting transfers between devices  12.2 us (4%)
  local copies, waits for them, and re-layouts  10.8 us (4%)
    all_gather x1, waiting for transfers between devices, on_device(): lax.all_gather(w_down, 'fsdp', axis=1, tiled=True)  96.8 us
    all_gather x1, waiting for transfers between devices, on_device(): lax.all_gather(w_up, 'fsdp', axis=0, tiled=True)  65.1 us
    pallas_call x1, Pallas kernels, tail(): pl.pallas_call(tail_kernel, out_shape=(jax.ShapeDtypeStruct((ROWS, COLS,...  37.4 us
    dot_general x1, matrix products, on_device(): lax.dot_general(d_pre, up_full, (((1,), (1,)), ((), ())), preferred_eleme...  13.3 us
    reduce_sum x1, other arithmetic, on_device(): mean_val = jnp.mean(conv, axis=-1, keepdims=True)  9.82 us
    ppermute x2, starting transfers between devices, with_halo(): before = lax.ppermute(last, axis, up)  8.87 us
    ppermute x2, waiting for transfers between devices, with_halo(): after = lax.ppermute(initial, axis, down)  8.07 us
    dot_general x1, matrix products, on_device(): jnp.dot(act.astype(jnp.bfloat16), down_full, preferred_element_type=jnp.f...  7.84 us
  transfers between devices with their start and end apart: 6, of which 5 were waited for; matrix products, arithmetic and copies ran while one was open for 10% of the time, Pallas kernels for 0%

profile of v1, /device:TPU:1, one launch (start us, length us, event | category | flops | bytes accessed | tf_op | source)
XLA Modules:
  0.0 296.6 jit_solution(5426187986830924223)
XLA Ops:
  7.2 0.0 all-gather.3.cloned.1.call-start
  7.2 0.7 all-gather.3.cloned.1.call-update
  7.9 0.0 all-gather.5.cloned.1.call-start
  7.9 0.7 all-gather.5.cloned.1.call-update
  8.6 0.0 copy-start.11
  8.7 0.9 exponential_bitcast_fusion
  9.5 0.1 copy.18
  9.7 0.3 mul.625
  10.0 0.0 copy-start
  10.0 0.1 mul.626
  10.1 0.0 copy-done.11
  10.1 0.1 multiply_convert_fusion.2
  10.2 0.0 copy-start.9
  10.3 4.5 %collective-permute-start = (bf16[1,3,16,1536]{3,2,1,0:T(8,128)(2,1)S(1)}, bf16[1,3,16,1536]{3,2,1,0:T(8,128)(2,1)S(1)}, u32[]{:S(2)}, u32[]{:S(2)}) collective-permute-start(bf16[1,3,16,1536]{3,2,1,0:T(8,128)(2,1)S(1)} %get-tuple-element.70), channel_id=1, source_target_pairs={{0,64},{64,128},{128,192},{1,65},{65,129},{129,193},{2,66},{66,130... | collective-permute-start | bytes 442376 | tf_op jit(solution)/shard_map/ppermute | solution.py:291
  14.8 1.9 collective-permute-start.1
  16.7 0.0 copy-done
  16.7 0.9 slice_reduce_fusion.47
  17.6 0.9 slice_reduce_fusion.48
  18.5 0.0 collective-permute-done
  18.5 2.7 collective-permute-done.1
  21.2 0.1 pad_maximum_fusion.3
  21.4 4.4 %collective-permute-start.2 = (bf16[1,14,3,1536]{3,2,1,0:T(4,128)(2,1)S(1)}, bf16[1,14,3,1536]{3,2,1,0:T(4,128)(2,1)S(1)}, u32[]{:S(2)}, u32[]{:S(2)}) collective-permute-start(bf16[1,14,3,1536]{3,2,1,0:T(4,128)(2,1)S(1)} %get-tuple-element.68), channel_id=1, source_target_pairs={{0,32},{1,33},{2,34},{3,35},{4,36},{5,37},{6,38},{7,39},{8,40},{9,... | collective-permute-start | bytes 387080 | tf_op jit(solution)/shard_map/ppermute | solution.py:291
  25.7 1.3 collective-permute-start.3
  27.0 0.8 slice_reduce_fusion.46
  27.8 0.2 collective-permute-done.2
  28.1 5.4 %collective-permute-done.3 = bf16[1,14,3,1536]{3,2,1,0:T(4,128)(2,1)S(1)} collective-permute-done((bf16[1,14,3,1536]{3,2,1,0:T(4,128)(2,1)S(1)}, bf16[1,14,3,1536]{3,2,1,0:T(4,128)(2,1)S(1)}, u32[]{:S(2)}, u32[]{:S(2)}) %collective-permute-start.3) | collective-permute-done | bytes 129056 | tf_op jit(solution)/shard_map/ppermute | solution.py:292
  33.5 0.5 pad_maximum_fusion
  33.9 0.0 copy-done.9
  33.9 1.7 convert_element_type.70
  35.8 0.0 copy-start.37
  35.8 0.0 copy-start.38
  35.8 0.0 copy-start.39
  35.8 0.0 copy-start.40
  35.9 2.6 copy.24
  38.5 0.0 copy-done.14
  38.8 9.8 %fusion.88 = (f32[8,16]{1,0:T(8,128)}, f32[8,16,1536]{2,1,0:T(8,128)S(1)}) fusion(f32[14,22,1536]{2,1,0:T(8,128)S(1)} %get-tuple-element.67, f32[1536]{0:T(1024)} %get-tuple-element.63, f32[1536]{0:T(1024)S(1)} %copy-done.19, f32[1536]{0:T(1024)S(1)} %copy-done.20, f32[1536]{0:T(1024)S(1)} %copy-done.21, f32[1536]{0:T(1024)S(1)} %copy-done.22, ...), kind=kLoop, calls=%fused_computation.209 | loop fusion | flops 19464064 | bytes 39629312 | tf_op jit(solution)/shard_map/reduce_sum | solution.py:329
  48.6 0.7 broadcast_multiply_fusion.1
  49.3 0.2 multiply_reduce_fusion.3
  49.5 0.0 copy-start.12
  49.5 0.0 copy-start.44
  49.5 0.0 copy-start.43
  49.5 1.9 pad_convert_fusion.xp
  51.4 0.9 add_convert_fusion.1
  52.4 65.1 %all-gather.3.cloned.1.call-done = bf16[1536,3072]{1,0:T(8,128)(2,1)} async-done(((bf16[48,3072]{1,0:T(8,128)(2,1)}), bf16[1536,3072]{1,0:T(8,128)(2,1)}) %all-gather.3.cloned.1.call-update) | async-done | bytes 9437200 | tf_op jit(solution)/shard_map/all_gather | solution.py:321
  117.5 0.0 copy-done.43
  117.5 6.4 %convolution_add_fusion = f32[128,3072]{1,0:T(8,128)} fusion(bf16[128,1536]{1,0:T(8,128)(2,1)} %bitcast.36, bf16[1536,3072]{1,0:T(8,128)(2,1)} %all-gather.3.cloned.1.call-done, f32[3072]{0:T(1024)S(1)} %copy-done.43), kind=kOutput, calls=%fused_computation | convolution fusion | flops 1208352768 | bytes 11415552 | tf_op jit(solution)/shard_map/dot_general | solution.py:334
  123.9 96.8 %all-gather.5.cloned.1.call-done = bf16[3072,1536]{0,1:T(8,128)(2,1)} async-done(((bf16[3072,48]{0,1:T(8,128)(2,1)}), bf16[3072,1536]{0,1:T(8,128)(2,1)}) %all-gather.5.cloned.1.call-update) | async-done | bytes 9437200 | tf_op jit(solution)/shard_map/all_gather | solution.py:322
  220.8 13.3 %multiply_reduce_fusion.2 = (f32[128]{0:T(128)S(1)}, f32[128,1536]{1,0:T(8,128)}) fusion(f32[1536]{0:T(1024)S(1)} %copy-done.12, bf16[1536,3072]{1,0:T(8,128)(2,1)} %all-gather.3.cloned.1.call-done, f32[128,3072]{1,0:T(8,128)} %convolution_add_fusion, bf16[3072,1536]{0,1:T(8,128)(2,1)} %all-gather.5.cloned.1.call-done, bf16[128,1536]{1,0:T(8,128)(2,1)} %bitcast.32, ...), kind=kOutput, calls=%fused_computation.123 | convolution fusion | flops 2424766464 | bytes 21639680 | tf_op jit(solution)/shard_map/dot_general | solution.py:346
  234.1 2.1 multiply_reduce_fusion
  236.2 0.0 copy-done.3
  236.2 0.1 copy-done.10
  236.3 7.8 %fusion.8 = (f32[1536]{0:T(1024)S(1)}, f32[128,1536]{1,0:T(8,128)}) fusion(bf16[1,8,16,1536]{3,2,1,0:T(8,128)(2,1)S(1)} %copy-done.3, f32[1536]{0:T(1024)S(1)} %copy-done.46, bf16[3072,1536]{0,1:T(8,128)(2,1)} %all-gather.5.cloned.1.call-done, f32[128,3072]{1,0:T(8,128)S(1)} %copy-done.10), kind=kOutput, calls=%fused_computation.19 | convolution fusion | flops 1212283392 | bytes 12201984 | tf_op jit(solution)/shard_map/dot_general | solution.py:336
  244.2 0.1 div.17
  244.3 1.7 bitcast_bitcast_fusion.dc
  246.1 37.4 %tail.1 = (bf16[8,16,1536]{2,1,0:T(8,128)(2,1)S(1)}, f32[7,7,1536]{2,1,0:T(8,128)S(1)}, f32[1,1536]{1,0:T(1,128)S(1)}, f32[1,1536]{1,0:T(1,128)S(1)}) custom-call(f32[12,16,32,128]{3,2,1,0:T(8,128)S(1)} %pad_convert_fusion.xp, f32[12,8,16,128]{3,2,1,0:T(8,128)S(1)} %bitcast_bitcast_fusion.dc, bf16[8,16,1536]{2,1,0:T(8,128)(2,1)S(1)} %bitcast.33, ...), custom_call_target="tpu_custom_call" | custom-call | tf_op jit(solution)/shard_map/tail/pallas_call | solution.py:253
  283.5 0.0 copy-start.1
  283.5 0.7 copy-done.1
  284.2 0.7 copy-done.5
  285.0 0.6 reduce.51
  285.6 0.6 reduce.52
  286.2 2.1 add_convert_fusion
  288.3 0.0 copy-done.2
  288.3 0.7 copy.27
  289.0 0.7 copy.28
  (80 shorter events, 0.2 us)
Async XLA Ops:
  7.2 110.4 %all-gather.3.cloned.1.call-start = ((), (), s32[]{:S(2)}) async-start(), calls=%async_computation | async-start | bytes 9732096 | tf_op jit(solution)/shard_map/all_gather | solution.py:321
  7.9 212.9 %all-gather.5.cloned.1.call-start = ((), (), s32[]{:S(2)}) async-start(), calls=%async_computation.1 | async-start | bytes 9732096 | tf_op jit(solution)/shard_map/all_gather | solution.py:322
  8.6 1.5 copy-start.11
  10.0 6.7 %copy-start = (f32[7,7,1536]{2,1,0:T(8,128)S(1)}, f32[7,7,1536]{2,1,0:T(8,128)}, u32[]{:S(2)}) copy-start(f32[7,7,1536]{2,1,0:T(8,128)} %taps.1) | copy-start | bytes 903172
  10.2 23.7 %copy-start.9 = (bf16[1,8,16,1536]{3,2,1,0:T(8,128)(2,1)}, bf16[1,8,16,1536]{3,2,1,0:T(8,128)(2,1)S(1)}, u32[]{:S(2)}) copy-start(bf16[1,8,16,1536]{3,2,1,0:T(8,128)(2,1)S(1)} %multiply_convert_fusion.2) | copy-start | bytes 1179652
  10.3 8.3 %collective-permute-start = (bf16[1,3,16,1536]{3,2,1,0:T(8,128)(2,1)S(1)}, bf16[1,3,16,1536]{3,2,1,0:T(8,128)(2,1)S(1)}, u32[]{:S(2)}, u32[]{:S(2)}) collective-permute-start(bf16[1,3,16,1536]{3,2,1,0:T(8,128)(2,1)S(1)} %get-tuple-element.70), channel_id=1, source_target_pairs={{0,64},{64,128},{128,192},{1,65},{65,129},{129,193},{2,66},{66,130... | collective-permute-start | bytes 442376 | tf_op jit(solution)/shard_map/ppermute | solution.py:291
  14.8 6.5 %collective-permute-start.1 = (bf16[1,3,16,1536]{3,2,1,0:T(8,128)(2,1)S(1)}, bf16[1,3,16,1536]{3,2,1,0:T(8,128)(2,1)S(1)}, u32[]{:S(2)}, u32[]{:S(2)}) collective-permute-start(bf16[1,3,16,1536]{3,2,1,0:T(8,128)(2,1)S(1)} %get-tuple-element.71), channel_id=1, source_target_pairs={{64,0},{128,64},{192,128},{65,1},{129,65},{193,129},{66,2},{130,66... | collective-permute-start | bytes 442376 | tf_op jit(solution)/shard_map/ppermute | solution.py:292
  21.4 6.7 %collective-permute-start.2 = (bf16[1,14,3,1536]{3,2,1,0:T(4,128)(2,1)S(1)}, bf16[1,14,3,1536]{3,2,1,0:T(4,128)(2,1)S(1)}, u32[]{:S(2)}, u32[]{:S(2)}) collective-permute-start(bf16[1,14,3,1536]{3,2,1,0:T(4,128)(2,1)S(1)} %get-tuple-element.68), channel_id=1, source_target_pairs={{0,32},{1,33},{2,34},{3,35},{4,36},{5,37},{6,38},{7,39},{8,40},{9,... | collective-permute-start | bytes 387080 | tf_op jit(solution)/shard_map/ppermute | solution.py:291
  25.7 7.7 %collective-permute-start.3 = (bf16[1,14,3,1536]{3,2,1,0:T(4,128)(2,1)S(1)}, bf16[1,14,3,1536]{3,2,1,0:T(4,128)(2,1)S(1)}, u32[]{:S(2)}, u32[]{:S(2)}) collective-permute-start(bf16[1,14,3,1536]{3,2,1,0:T(4,128)(2,1)S(1)} %get-tuple-element.69), channel_id=1, source_target_pairs={{32,0},{33,1},{34,2},{35,3},{36,4},{37,5},{38,6},{39,7},{40,8},{41... | collective-permute-start | bytes 387080 | tf_op jit(solution)/shard_map/ppermute | solution.py:292
  35.6 2.9 copy-start.13
  35.6 2.9 copy-start.14
  35.6 2.9 copy-start.15
  35.6 2.9 copy-start.16
  35.6 2.9 copy-start.17
  35.6 2.9 copy-start.18
  35.6 2.9 copy-start.19
  35.6 2.9 copy-start.20
  35.6 2.9 copy-start.21
  35.7 2.9 copy-start.22
  35.7 2.9 copy-start.23
  35.7 2.9 copy-start.24
  35.7 2.9 copy-start.25
  35.7 2.9 copy-start.26
  35.7 2.9 copy-start.27
  35.7 2.9 copy-start.28
  35.7 2.9 copy-start.29
  35.7 2.9 copy-start.30
  35.7 2.9 copy-start.31
  35.8 2.9 copy-start.32
  35.8 2.9 copy-start.33
  35.8 2.9 copy-start.34
  35.8 2.9 copy-start.35
  35.8 2.9 copy-start.36
  35.8 2.9 copy-start.37
  35.8 2.9 copy-start.38
  35.8 2.9 copy-start.39
  35.8 2.9 copy-start.40
  35.9 2.9 copy-start.41
  35.9 2.9 copy-start.42
  48.6 0.9 copy-start.7
  49.5 1.9 copy-start.8
  49.5 1.9 copy-start.12
  49.5 1.9 copy-start.44
  49.5 68.0 %copy-start.43 = (f32[3072]{0:T(1024)S(1)}, f32[3072]{0:T(1024)}, u32[]{:S(2)}) copy-start(f32[3072]{0:T(1024)} %param.19) | copy-start | bytes 36868
  117.5 103.2 %copy-start.45 = (f32[1536]{0:T(1024)S(1)}, f32[1536]{0:T(1024)}, u32[]{:S(2)}) copy-start(f32[1536]{0:T(1024)} %param.22) | copy-start | bytes 18436
  234.1 2.1 copy-start.3
  234.1 2.2 copy-start.10
  234.1 2.2 copy-start.46
  244.3 1.8 copy-start.4
  283.5 0.7 copy-start.1
  284.2 0.7 copy-start.5
  285.0 3.3 %copy-start.2 = (bf16[8,16,1536]{2,1,0:T(8,128)(2,1)S(1)}, bf16[8,16,1536]{2,1,0:T(8,128)(2,1)}, u32[]{:S(2)}) copy-start(bf16[8,16,1536]{2,1,0:T(8,128)(2,1)} %copy-done.1) | copy-start | bytes 1179652
  285.0 4.1 %copy-start.6 = (f32[7,7,1536]{2,1,0:T(8,128)S(1)}, f32[7,7,1536]{2,1,0:T(8,128)}, u32[]{:S(2)}) copy-start(f32[7,7,1536]{2,1,0:T(8,128)} %copy-done.5) | copy-start | bytes 903172
Sparse Core Ops, SparseCore 0:
  10.6 106.9 all-gather.2
  120.1 100.5 all-gather.4

commit v2 on v1

--- a/solution.py
+++ b/solution.py
@@ -1,5 +1,3 @@
-import functools
-
 import jax
 import jax.numpy as jnp
 from jax import lax
@@ -13,6 +11,8 @@
 ROWS, COLS, CHANS = 8, 16, 1536
 PR, PC = 16, 32
 PIECE = 11
+HID = 1536
+GELU_C = 0.7978845608028654
 MESH = pl.DeviceIdType.MESH
 
 
@@ -107,18 +107,41 @@
             grads[b * 7 + i, j, :] = jnp.sum(q, axis=0)
 
 
-def tail_kernel(
-    xp, dc, cot, taps, extra, gi, gk, gg, gs,
-    gp, stage, landed, grads, got1, part, got2, fin, full,
+TOK = ROWS * COLS
+
+
+def block_kernel(
+    code, expo, cot, taps, dw_bias, ln_gain, ln_bias, w_up, b_up, w_down, b_down, layer_scale,
+    bo, gi, gk, gg, gs,
+    xp, gp, stage, landed, up, down, ln, dm, conv, rstd, pre, dact, act, dpre,
+    mine_dln, send_dln, got_dln, mine_mlp, send_mlp, got_mlp,
+    grads, got1, part, got2, fin, full,
+    ls, a1s, a1r, azs, azr, bzs, bzr, bys, byr, bfs, bfr, ts, tr, dls, dlr, mls, mlr,
     hs, hr, cs, cr, s1, r1, s2, r2, s3, r3, s4, r4,
 ):
     sx, sy, f = lax.axis_index("sx"), lax.axis_index("sy"), lax.axis_index("fsdp")
     g = sx * 2 + sy
+    half = lax.rem(sx, 2)
+    other = {"sx": sx + 1 - 2 * half}
+    z, y = f // 4, lax.rem(f, 4)
+    f32, bf16 = jnp.float32, jnp.bfloat16
 
     def peer(k):
         p = lax.rem(g + k, 8)
         return p, {"sx": p // 2, "sy": lax.rem(p, 2)}
 
+    def zz(d):
+        return lax.rem(z + d + 8, 8)
+
+    def yy(d):
+        return lax.rem(y + d + 4, 4)
+
+    def shard(buf, dz, dy):
+        return buf.at[pl.ds(pl.multiple_of((zz(dz) * 4 + yy(dy)) * 48, 16), 48)]
+
+    def pair(buf, dz, q):
+        return buf.at[pl.ds(pl.multiple_of((zz(dz) * 4 + 2 * q) * 48, 16), 96)]
+
     barrier = pltpu.get_barrier_semaphore()
     for k in range(1, 8):
         pl.semaphore_signal(barrier, inc=1, device_id=peer(k)[1], device_id_type=MESH)
@@ -127,31 +150,263 @@
     def _(k):
         pl.semaphore_signal(barrier, inc=1, device_id={"fsdp": lax.rem(f + k, 32)}, device_id_type=MESH)
 
-    gp[:, 3:11, 8:24, :] = dc[...]
+    hidden = pl.ds(pl.multiple_of(half * HID, HID), HID)
+    own = [
+        pltpu.make_async_copy(w_up.at[:, hidden], shard(up, 0, 0), ls.at[0]),
+        pltpu.make_async_copy(w_down.at[:, hidden], shard(down, 0, 0), ls.at[1]),
+    ]
+    for copy in own:
+        copy.start()
+    for copy in own:
+        copy.wait()
+    pl.semaphore_wait(barrier, 38)
+
+    sent = []
+
+    def send(copy):
+        copy.start()
+        sent.append(copy)
+
+    def up_y(k):
+        return remote(shard(up, 0, 0), shard(up, 0, 0), a1s.at[k - 1], a1r.at[k - 1], {"fsdp": z * 4 + yy(k)})
+
+    def up_y_got(k):
+        return remote(shard(up, 0, -k), shard(up, 0, -k), a1s.at[k - 1], a1r.at[k - 1], {"fsdp": z * 4 + yy(k)})
+
+    def up_z(way, q, s, got=False):
+        sign = 1 - 2 * way
+        block = pair(up, -sign * (s if got else s - 1), q)
+        at = way * 8 + q * 4 + s - 1
+        return remote(block, block, azs.at[at], azr.at[at], {"fsdp": zz(sign) * 4 + y})
+
+    def up_z_steps(s):
+        return [(way, q) for way in (0, 1) for q in (0, 1) if s <= (4 if way == q else 3)]
+
+    def down_z(way, s, got=False):
+        sign = 1 - 2 * way
+        block = shard(down, -sign * (s if got else s - 1), 0)
+        at = way * 4 + s - 1
+        return remote(block, block, bzs.at[at], bzr.at[at], {"fsdp": zz(sign) * 4 + y})
+
+    def down_y(way, d, got=False):
+        sign = 1 - 2 * way
+        block = shard(down, d, -sign if got else 0)
+        at = way * 8 + d
+        return remote(block, block, bys.at[at], byr.at[at], {"fsdp": z * 4 + yy(sign)})
+
+    def down_on(d, got=False):
+        sign = 1 - 2 * (d % 2)
+        block = shard(down, d, 2 if got else -sign)
+        return remote(block, block, bfs.at[d], bfr.at[d], {"fsdp": z * 4 + yy(sign)})
+
+    def step_down_z(s):
+        for way in (0, 1):
+            if s <= 4 - way:
+                down_z(way, s, True).wait_recv()
+                if s + 1 <= 4 - way:
+                    send(down_z(way, s + 1))
+                d = (8 - s) if way == 0 else s
+                send(down_y(0, d))
+                send(down_y(1, d))
+
+    def step_down_y(d):
+        down_y(0, d, True).wait_recv()
+        down_y(1, d, True).wait_recv()
+        send(down_on(d))
+
+    def step_up_z(s):
+        for way, q in up_z_steps(s):
+            up_z(way, q, s, True).wait_recv()
+            if (way, q) in up_z_steps(s + 1):
+                send(up_z(way, q, s + 1))
+
+    for k in (1, 3, 2):
+        send(up_y(k))
+    send(down_z(0, 1))
+    send(down_z(1, 1))
+    send(down_y(0, 0))
+    send(down_y(1, 0))
+
+    factor = jnp.left_shift(1, expo[...] + 2).astype(f32) * 0.25
+    for b in range(NB):
+        at = slice(b * 128, (b + 1) * 128)
+        scaled = code[:, :, at].astype(f32) * factor[:, :, b : b + 1]
+        xp[b, 3:11, 8:24, :] = scaled
+    zero_rows(xp, sx)
+    row_halo(xp, hs.at[0], hr.at[0], sx, "start")
+
+    @pl.loop(0, NB)
+    def _(b):
+        ct = cot[:, :, lanes(b)].astype(f32).reshape(TOK, 128)
+        dm[0:TOK, lanes(b)] = (layer_scale[:, lanes(b)] * ct).astype(bf16)
+
+    def tokens(buf, at):
+        return remote(buf.at[0:TOK], buf.at[TOK : 2 * TOK], ts.at[at], tr.at[at], other)
+
+    send(tokens(dm, 0))
+
+    for k in (1, 3, 2):
+        up_y_got(k).wait_recv()
+    for way, q in up_z_steps(1):
+        send(up_z(way, q, 1))
+    step_down_z(1)
+    row_halo(xp, hs.at[0], hr.at[0], sx, "wait")
+    pack_cols(xp, stage.at[0], sy)
+    xcol = remote(stage.at[0], landed.at[0], cs.at[0], cr.at[0], {"sy": 1 - sy})
+    xcol.start()
+    step_down_y(0)
     zero_rows(gp, sx)
-    grads[84:88] = jnp.zeros((4, 8, 128), jnp.float32)
-    pl.semaphore_wait(barrier, 38)
-
-    row_halo(gp, hs, hr, sx, "start")
+    grads[84:88] = jnp.zeros((4, 8, 128), f32)
+    xcol.wait()
+    unpack_cols(xp, landed.at[0], sy)
+
+    def forward_conv(b):
+        start = jnp.broadcast_to(dw_bias[:, lanes(b)].reshape(1, 1, 128), (ROWS, COLS, 128))
+        conv[b] = depthwise(xp, b, taps, start, False).reshape(TOK, 128)
+
+    pl.loop(0, NB)(forward_conv)
+    step_down_z(2)
+
+    def over_channels(term):
+        total = lax.fori_loop(0, NB, lambda b, t: t + term(b), jnp.zeros((TOK, 128), f32))
+        return jnp.sum(total, axis=1, keepdims=True) / CHANS
+
+    mu = over_channels(lambda b: conv[b])
+    var = over_channels(lambda b: (conv[b] - mu) * (conv[b] - mu))
+    rstd[...] = jnp.broadcast_to(lax.rsqrt(var + 1e-6), (TOK, 128))
+
+    @pl.loop(0, NB)
+    def _(b):
+        normed = (conv[b] - mu) * rstd[...]
+        conv[b] = normed
+        ln[0:TOK, lanes(b)] = (normed * ln_gain[:, lanes(b)] + ln_bias[:, lanes(b)]).astype(bf16)
+
+    send(tokens(ln, 1))
+    step_down_y(7)
+    step_down_y(1)
+    step_up_z(1)
+    step_down_z(3)
+    tokens(dm, 0).wait_recv()
+    tokens(ln, 1).wait_recv()
+
+    odd = lax.rem(z, 2)
+
+    def tile(n):
+        return pl.ds(pl.multiple_of(n * 256, 256), 256)
+
+    def add_pre(s):
+        base = (-odd, -2 + 3 * odd, 2 - 5 * odd, 4 - odd)[s - 1]
+        rows = pl.ds(pl.multiple_of(zz(base) * 192, 384), 384)
+
+        @pl.loop(0, 6)
+        def _(n):
+            term = jnp.dot(ln[:, rows], up[rows, tile(n)], preferred_element_type=f32)
+            if s == 1:
+                start = pl.multiple_of(half * HID + n * 256, 256)
+                pre[:, tile(n)] = term + b_up[:, pl.ds(start, 256)]
+            else:
+                pre[:, tile(n)] = pre[:, tile(n)] + term
+
+    add_pre(1)
+    step_down_y(6)
+    step_down_y(2)
+    step_up_z(2)
+    step_down_z(4)
+    add_pre(2)
+    step_down_y(5)
+    step_down_y(3)
+    step_up_z(3)
+    step_down_y(4)
+    add_pre(3)
+    for d in range(8):
+        down_on(d, True).wait_recv()
+
+    @pl.loop(0, 6)
+    def _(n):
+        dact[:, tile(n)] = jnp.dot(dm[...], down[:, tile(n)], preferred_element_type=f32)
+
+    step_up_z(4)
+    add_pre(4)
+
+    @pl.loop(0, 12)
+    def _(n):
+        v = pre[:, lanes(n)]
+        v2 = v * v
+        t = jnp.tanh(GELU_C * v * (1.0 + 0.044715 * v2))
+        cdf = 0.5 * (1.0 + t)
+        act[:, lanes(n)] = (v * cdf).astype(bf16)
+        slope = cdf + 0.5 * v * (1.0 - t * t) * (GELU_C * (1.0 + 3 * 0.044715 * v2))
+        dpre[:, lanes(n)] = (dact[:, lanes(n)] * slope).astype(bf16)
+
+    moved_dln = (send_dln, got_dln, dls, dlr)
+    moved_mlp = (send_mlp, got_mlp, mls, mlr)
+
+    def arrived(moved, n):
+        src, dst, sends, recvs = moved
+        return remote(src.at[:, tile(n)], dst.at[:, tile(n)], sends.at[n], recvs.at[n], other)
+
+    def down_projection(lhs, weights, mine, moved):
+        @pl.loop(0, 6)
+        def _(n):
+            out = lax.dot_general(
+                lhs[...], weights[tile(n), :], (((1,), (1,)), ((), ())), preferred_element_type=f32
+            )
+            mine[:, tile(n)] = out[0:TOK]
+            moved[0][:, tile(n)] = out[TOK : 2 * TOK]
+            arrived(moved, n).start()
+
+    down_projection(dpre, up, mine_dln, moved_dln)
+    down_projection(act, down, mine_mlp, moved_mlp)
+
+    def back_sums(b, sums):
+        @pl.when(lax.rem(b, 2) == 0)
+        def _():
+            arrived(moved_dln, b // 2).wait_recv()
+
+        d_ln = mine_dln[:, lanes(b)] + got_dln[:, lanes(b)]
+        grads[b * 7, 7, :] = jnp.sum(d_ln * conv[b], axis=0)
+        d_norm = d_ln * ln_gain[:, lanes(b)]
+        mine_dln[:, lanes(b)] = d_norm
+        return sums[0] + d_norm, sums[1] + d_norm * conv[b]
+
+    zeros = jnp.zeros((TOK, 128), f32)
+    sum_d, sum_dn = lax.fori_loop(0, NB, back_sums, (zeros, zeros))
+    mean_d = jnp.sum(sum_d, axis=1, keepdims=True) / CHANS
+    mean_dn = jnp.sum(sum_dn, axis=1, keepdims=True) / CHANS
+
+    @pl.loop(0, NB)
+    def _(b):
+        d_conv = rstd[...] * (mine_dln[:, lanes(b)] - mean_d - conv[b] * mean_dn)
+        gp[b, 3:11, 8:24, :] = d_conv.reshape(ROWS, COLS, 128)
+
+    row_halo(gp, hs.at[1], hr.at[1], sx, "start")
+
+    @pl.loop(0, NB)
+    def _(b):
+        @pl.when(lax.rem(b, 2) == 0)
+        def _():
+            arrived(moved_mlp, b // 2).wait_recv()
+
+        mlp = (mine_mlp[:, lanes(b)] + got_mlp[:, lanes(b)]) + b_down[:, lanes(b)]
+        ct = cot[:, :, lanes(b)].astype(jnp.float32).reshape(TOK, 128)
+        grads[b * 7 + 1, 7, :] = jnp.sum(ct * mlp, axis=0)
+        scaled = xp[b, 3:11, 8:24, :].reshape(TOK, 128)
+        bo[:, lanes(b)] = (scaled + layer_scale[:, lanes(b)] * mlp).astype(jnp.bfloat16)
+        for i in range(2, 7):
+            grads[b * 7 + i, 7, :] = jnp.zeros((128,), jnp.float32)
 
     @pl.loop(0, 6)
     def _(b):
         kernel_grad(xp, gp, grads, b)
 
-    row_halo(gp, hs, hr, sx, "wait")
-    pack_cols(gp, stage, sy)
-    col = remote(stage, landed, cs, cr, {"sy": 1 - sy})
+    row_halo(gp, hs.at[1], hr.at[1], sx, "wait")
+    pack_cols(gp, stage.at[1], sy)
+    col = remote(stage.at[1], landed.at[1], cs.at[1], cr.at[1], {"sy": 1 - sy})
     col.start()
 
     @pl.loop(6, NB)
     def _(b):
         kernel_grad(xp, gp, grads, b)
-
-    for b in range(NB):
-        grads[b * 7, 7, :] = extra[0, b * 128 : (b + 1) * 128]
-        grads[b * 7 + 1, 7, :] = extra[1, b * 128 : (b + 1) * 128]
-        for i in range(2, 7):
-            grads[b * 7 + i, 7, :] = jnp.zeros((128,), jnp.float32)
 
     first = []
     for k in range(1, 8):
@@ -160,7 +415,7 @@
         first[-1].start()
 
     col.wait()
-    unpack_cols(gp, landed, sy)
+    unpack_cols(gp, landed.at[1], sy)
 
     def out_conv(b):
         gi[:, :, lanes(b)] = depthwise(
@@ -245,122 +500,66 @@
         def _(k):
             spread(k).wait_send()
 
-
-def tail(xp, dc, cot, taps, extra):
+    for n in range(6):
+        arrived(moved_dln, n).wait_send()
+        arrived(moved_mlp, n).wait_send()
+    for copy in sent:
+        copy.wait_send()
+
+
+def on_device(
+    x_code, x_exp, dw_kernel, dw_bias, ln_gain, ln_bias, w_up, b_up, w_down, b_down, layer_scale, cotangent
+):
     vmem = pl.BlockSpec(memory_space=pltpu.VMEM)
+    anywhere = pl.BlockSpec(memory_space=pl.ANY)
     dma = pltpu.SemaphoreType.DMA
     f32, bf16 = jnp.float32, jnp.bfloat16
-    return pl.pallas_call(
-        tail_kernel,
+    row = lambda v: v.reshape(1, -1)
+    tok_f32 = pltpu.VMEM((TOK, CHANS), f32)
+    pair_f32, pair_bf16 = pltpu.VMEM((2 * TOK, HID), f32), pltpu.VMEM((2 * TOK, HID), bf16)
+    weight = pltpu.VMEM((CHANS, HID), bf16)
+    padded = pltpu.VMEM((NB, PR, PC, 128), f32)
+    staged = pltpu.VMEM((2, 3, NB * 16, 128), bf16)
+    block_out, grad_input, grad_kernel, grad_gain, grad_scale = pl.pallas_call(
+        block_kernel,
         out_shape=(
+            jax.ShapeDtypeStruct((TOK, CHANS), bf16),
             jax.ShapeDtypeStruct((ROWS, COLS, CHANS), bf16),
             jax.ShapeDtypeStruct((KW, KW, CHANS), f32),
             jax.ShapeDtypeStruct((1, CHANS), f32),
             jax.ShapeDtypeStruct((1, CHANS), f32),
         ),
-        in_specs=[vmem] * 5,
-        out_specs=(vmem,) * 4,
+        in_specs=[vmem] * 7 + [anywhere, vmem, anywhere, vmem, vmem],
+        out_specs=(vmem,) * 5,
         scratch_shapes=[
-            pltpu.VMEM((NB, PR, PC, 128), f32),
-            pltpu.VMEM((3, NB * 16, 128), bf16),
-            pltpu.VMEM((3, NB * 16, 128), bf16),
+            padded, padded, staged, staged, weight, weight, pair_bf16, pair_bf16,
+            pltpu.VMEM((NB, TOK, 128), f32), pltpu.VMEM((TOK, 128), f32),
+            pair_f32, pair_f32, pair_bf16, pair_bf16,
+            tok_f32, tok_f32, tok_f32, tok_f32, tok_f32, tok_f32,
             pltpu.VMEM((88, 8, 128), f32),
             pltpu.VMEM((7, PIECE, 8, 128), f32),
             pltpu.VMEM((PIECE, 8, 128), f32),
             pltpu.VMEM((32, 8, 128), f32),
             pltpu.VMEM((PIECE, 8, 128), f32),
             pltpu.VMEM((88, 8, 128), f32),
-            dma((2,)), dma((2,)), dma, dma,
+            dma((2,)), dma((3,)), dma((3,)), dma((16,)), dma((16,)), dma((8,)), dma((8,)),
+            dma((16,)), dma((16,)), dma((8,)), dma((8,)), dma((2,)), dma((2,)),
+            dma((6,)), dma((6,)), dma((6,)), dma((6,)),
+            dma((2, 2)), dma((2, 2)), dma((2,)), dma((2,)),
             dma((7,)), dma((7,)), dma((PIECE,)), dma((32,)),
             dma((32,)), dma((PIECE,)), dma((7,)), dma((7,)),
         ],
         compiler_params=pltpu.CompilerParams(
-            collective_id=1, has_side_effects=True, vmem_limit_bytes=40 * 2**20
+            collective_id=1, has_side_effects=True, vmem_limit_bytes=56 * 2**20
         ),
-        name="tail",
-    )(xp, dc, cot, taps, extra)
-
-
-def with_halo(shard, sides, width):
-    for axis, dim in sides:
-        devices, length = (lax.axis_size(axis), shard.shape[dim])
-        up = [(i, (i + 1) % devices) for i in range(devices - 1)]
-        down = [(j, i) for i, j in up]
-        last = lax.slice_in_dim(shard, length - width, length, axis=dim)
-        initial = lax.slice_in_dim(shard, 0, width, axis=dim)
-        before = lax.ppermute(last, axis, up)
-        after = lax.ppermute(initial, axis, down)
-        shard = jnp.concatenate([before, shard, after], axis=dim)
-    return shard
-
-
-def gelu_tanh(v):
-    return jax.nn.gelu(v, approximate=True)
-
-
-def on_device(
-    x_code,
-    x_exp,
-    dw_kernel,
-    dw_bias,
-    ln_gain,
-    ln_bias,
-    w_up,
-    b_up,
-    w_down,
-    b_down,
-    layer_scale,
-    cotangent,
-):
-    code = x_code[0]
-    rows, cols, chans = code.shape
-    factor = jnp.exp2(x_exp[0].astype(jnp.float32))
-    grouped = code.astype(jnp.float32).reshape(rows, cols, chans // CG, CG) * factor[..., None]
-    scaled = grouped.reshape(rows, cols, chans).astype(jnp.bfloat16)
-    up_full, down_full = (
-        lax.all_gather(w_up, "fsdp", axis=0, tiled=True),
-        lax.all_gather(w_down, "fsdp", axis=1, tiled=True),
+        name="block",
+    )(
+        x_code[0], x_exp[0], cotangent[0], dw_kernel, row(dw_bias), row(ln_gain), row(ln_bias),
+        w_up, row(b_up), w_down.T, row(b_down), row(layer_scale),
     )
-    padded_x = with_halo(scaled[None], (("sx", 1), ("sy", 2)), 3)[0].astype(jnp.float32)
-    conv = jnp.zeros((rows, cols, chans), jnp.float32) + dw_bias
-    for i in range(KW):
-        for j in range(KW):
-            conv = conv + dw_kernel[i, j] * padded_x[i : i + rows, j : j + cols]
-    mean_val = jnp.mean(conv, axis=-1, keepdims=True)
-    centred = conv - mean_val
-    rstd = lax.rsqrt(jnp.mean(centred * centred, axis=-1, keepdims=True) + 1e-06)
-    normed = centred * rstd
-    ln_out = (normed * ln_gain + ln_bias).astype(jnp.bfloat16).reshape(rows * cols, chans)
-    pre = jnp.dot(ln_out, up_full, preferred_element_type=jnp.float32) + b_up
-    act, gelu_back = jax.vjp(gelu_tanh, pre)
-    mlp = jnp.dot(act.astype(jnp.bfloat16), down_full, preferred_element_type=jnp.float32) + b_down
-    mlp = mlp.reshape(rows, cols, chans)
-    block_out = (scaled.astype(jnp.float32) + layer_scale * mlp).astype(jnp.bfloat16)
-    grad_f = cotangent[0].astype(jnp.float32)
-    scale_term = jnp.sum(grad_f * mlp, axis=(0, 1))
-    d_mlp = (layer_scale * grad_f).astype(jnp.bfloat16).reshape(rows * cols, chans)
-    d_act = lax.dot_general(
-        d_mlp, down_full, (((1,), (1,)), ((), ())), preferred_element_type=jnp.float32
+    return (
+        block_out.reshape(1, ROWS, COLS, CHANS), grad_input[None], grad_kernel, grad_gain[0], grad_scale[0]
     )
-    d_pre = gelu_back(d_act)[0].astype(jnp.bfloat16)
-    d_ln = lax.dot_general(
-        d_pre, up_full, (((1,), (1,)), ((), ())), preferred_element_type=jnp.float32
-    )
-    d_ln = d_ln.reshape(rows, cols, chans)
-    gain_term = jnp.sum(d_ln * normed, axis=(0, 1))
-    d_norm = d_ln * ln_gain
-    d_conv = rstd * (
-        d_norm
-        - jnp.mean(d_norm, axis=-1, keepdims=True)
-        - normed * jnp.mean(d_norm * normed, axis=-1, keepdims=True)
-    )
-    blocked_x = padded_x.reshape(rows + 6, cols + 6, NB, 128).transpose(2, 0, 1, 3)
-    blocked_x = jnp.pad(blocked_x, ((0, 0), (0, 2), (5, 5), (0, 0)))
-    blocked_g = d_conv.reshape(rows, cols, NB, 128).transpose(2, 0, 1, 3)
-    grad_input, grad_kernel, grad_gain, grad_scale = tail(
-        blocked_x, blocked_g, cotangent[0], dw_kernel, jnp.stack([gain_term, scale_term])
-    )
-    return (block_out[None], grad_input[None], grad_kernel, grad_gain[0], grad_scale[0])
 
 
 def solution(mesh):

time: 297 us -> 135 us (0.45)
  waiting for transfers between devices: 172 us -> 0 us
  Pallas kernels: 37.4 us -> 122 us
  matrix products: 27.6 us -> 0 us
  other arithmetic: 22.2 us -> 1.24 us
  between operations: 14.8 us -> 0.67 us
  starting transfers between devices: 12.2 us -> 0 us
    all_gather x2 -> x0, waiting for transfers between devices: 162 us -> none  [the longest x1 96.8 us: on_device(): lax.all_gather(w_down, 'fsdp', axis=1, tiled=True)]
    pallas_call x1, Pallas kernels: 37.4 us -> 122 us  [on_device(): pl.pallas_call(block_kernel, out_shape=(jax.ShapeDtypeStruct((TOK, CHANS)...]
    dot_general x3 -> x0, matrix products: 27.6 us -> none  [the longest x1 13.3 us: on_device(): lax.dot_general(d_pre, up_full, (((1,), (1,)), ((), ())), preferred_eleme...]
    reduce_sum x3 -> x0, other arithmetic: 12.1 us -> none  [the longest x1 9.82 us: on_device(): mean_val = jnp.mean(conv, axis=-1, keepdims=True)]
    ppermute x4 -> x0, starting transfers between devices: 12.1 us -> none  [the longest x2 8.87 us: with_halo(): before = lax.ppermute(last, axis, up)]
    ppermute x4 -> x0, waiting for transfers between devices: 8.32 us -> none  [the longest x2 8.07 us: with_halo(): after = lax.ppermute(initial, axis, down)]
    reshape x0 -> x5, local copies, waits for them, and re-layouts: none -> 5.8 us  [on_device(): row = lambda v: v.reshape(1, -1)]
    convert_element_type x2 -> x0, local copies, waits for them, and re-layouts: 4.28 us -> none  [on_device(): with_halo(scaled[None], (('sx', 1), ('sy', 2)), 3)[0].astype(jnp.float32)]
  transfers between devices with their start and end apart: 6 -> 0, of which waited for: 5 -> 0; matrix products, arithmetic and copies ran while one was open for 10% -> 0% of each run, Pallas kernels for 0% -> 0%
where the time goes in v2:
time: 135 us
  Pallas kernels  122 us (90%)
  local copies, waits for them, and re-layouts  11 us (8%)
    pallas_call x1, Pallas kernels, on_device(): pl.pallas_call(block_kernel, out_shape=(jax.ShapeDtypeStruct((TOK, CHANS)...  122 us
    reshape x5, local copies, waits for them, and re-layouts, on_device(): row = lambda v: v.reshape(1, -1)  5.8 us
    unnamed x16, local copies, waits for them, and re-layouts  5.19 us

profile of v2, /device:TPU:1, one launch (start us, length us, event | category | flops | bytes accessed | tf_op | source)
XLA Modules:
  0.0 135.0 jit_solution(6454616043008058021)
XLA Ops:
  0.6 0.0 copy-start.2
  0.6 1.3 reshape.31.dw_bias
  1.9 1.3 reshape.32.ln_gain
  3.2 1.3 reshape.33.ln_bias
  4.5 0.0 copy-start.3
  4.5 1.3 reshape.35.b_down
  5.8 0.0 copy-done.3
  5.8 0.6 reshape.36.layer_scale
  6.4 0.0 copy-done.2
  6.5 0.8 copy.17
  7.2 122.1 %block.1 = (bf16[128,1536]{1,0:T(8,128)(2,1)}, bf16[8,16,1536]{2,1,0:T(8,128)(2,1)}, f32[7,7,1536]{2,1,0:T(8,128)}, f32[1,1536]{1,0:T(1,128)}, f32[1,1536]{1,0:T(1,128)}) custom-call(bf16[8,16,1536]{2,1,0:T(8,128)(2,1)} %bitcast.9, s32[8,16,12]{2,1,0:T(8,128)} %bitcast.12, bf16[8,16,1536]{2,1,0:T(8,128)(2,1)} %bitcast.10, f32[7,7,1536]{2,1,0:T(8,128)} %taps.1, ...), custom_call_target="tpu_custom_call" | custom-call | tf_op jit(solution)/shard_map/block/pallas_call | solution.py:523
  129.3 0.0 copy-start.5
  129.3 0.7 copy-done.5
  130.0 0.0 copy-start.4
  130.0 0.6 reduce
  130.6 0.1 copy-done.4
  130.7 0.6 reduce.1
  131.3 0.0 copy-start
  131.3 1.8 %copy.21 = bf16[1,8,16,1536]{3,2,1,0:T(8,128)(2,1)} copy(bf16[1,8,16,1536]{3,2,1,0:T(8,128)(2,1)} %bitcast.8) | data formatting | bytes 786432
  133.1 0.0 copy-done
  133.1 0.0 copy-start.1
  133.1 0.7 copy.22
  133.9 0.4 copy-done.1
  134.3 0.7 copy.23
Async XLA Ops:
  0.6 5.8 %copy-start.2 = (s32[1,8,16,12]{2,1,3,0:T(8,128)S(1)}, s32[1,8,16,12]{2,1,3,0:T(8,128)}, u32[]{:S(2)}) copy-start(s32[1,8,16,12]{2,1,3,0:T(8,128)} %param.13) | copy-start | bytes 18436
  4.5 1.3 copy-start.3
  129.3 0.7 copy-start.5
  130.0 0.7 copy-start.4
  131.3 1.8 %copy-start = (bf16[8,16,1536]{2,1,0:T(8,128)(2,1)S(1)}, bf16[8,16,1536]{2,1,0:T(8,128)(2,1)}, u32[]{:S(2)}) copy-start(bf16[8,16,1536]{2,1,0:T(8,128)(2,1)} %get-tuple-element.11) | copy-start | bytes 1179652
  133.1 1.1 copy-start.1

commit v3 on v2

--- a/solution.py
+++ b/solution.py
@@ -111,12 +111,12 @@
 
 
 def block_kernel(
-    code, expo, cot, taps, dw_bias, ln_gain, ln_bias, w_up, b_up, w_down, b_down, layer_scale,
+    code, expo, cot, taps, dw_bias_in, ln_gain_in, ln_bias_in, w_up, b_up, w_down, b_down_in, layer_scale_in,
     bo, gi, gk, gg, gs,
-    xp, gp, stage, landed, up, down, ln, dm, conv, rstd, pre, dact, act, dpre,
+    dw_bias, ln_gain, ln_bias, b_down, layer_scale, xp, gp, stage, landed, up, down, ln, dm, conv, rstd, pre, dact, act, dpre,
     mine_dln, send_dln, got_dln, mine_mlp, send_mlp, got_mlp,
     grads, got1, part, got2, fin, full,
-    ls, a1s, a1r, azs, azr, bzs, bzr, bys, byr, bfs, bfr, ts, tr, dls, dlr, mls, mlr,
+    ls, vs, xus, xur, xds, xdr, a1s, a1r, azs, azr, bzs, bzr, bys, byr, bfs, bfr, ts, tr, dls, dlr, mls, mlr,
     hs, hr, cs, cr, s1, r1, s2, r2, s3, r3, s4, r4,
 ):
     sx, sy, f = lax.axis_index("sx"), lax.axis_index("sy"), lax.axis_index("fsdp")
@@ -130,6 +130,14 @@
         p = lax.rem(g + k, 8)
         return p, {"sx": p // 2, "sy": lax.rem(p, 2)}
 
+    x = sy * 2 + sx // 2
+    odd_x = lax.rem(x, 2)
+    window = pl.ds(pl.multiple_of(odd_x * 512, 512), 1024)
+
+    def x_peer(sign):
+        to = lax.rem(x + sign + 4, 4)
+        return {"sx": lax.rem(to, 2) * 2 + half, "sy": to // 2}
+
     def zz(d):
         return lax.rem(z + d + 8, 8)
 
@@ -137,29 +145,32 @@
         return lax.rem(y + d + 4, 4)
 
     def shard(buf, dz, dy):
-        return buf.at[pl.ds(pl.multiple_of((zz(dz) * 4 + yy(dy)) * 48, 16), 48)]
+        return buf.at[pl.ds(pl.multiple_of((zz(dz) * 4 + yy(dy)) * 48, 16), 48), window]
 
     def pair(buf, dz, q):
-        return buf.at[pl.ds(pl.multiple_of((zz(dz) * 4 + 2 * q) * 48, 16), 96)]
+        return buf.at[pl.ds(pl.multiple_of((zz(dz) * 4 + 2 * q) * 48, 16), 96), window]
 
     barrier = pltpu.get_barrier_semaphore()
-    for k in range(1, 8):
-        pl.semaphore_signal(barrier, inc=1, device_id=peer(k)[1], device_id_type=MESH)
-
-    @pl.loop(1, 32)
-    def _(k):
-        pl.semaphore_signal(barrier, inc=1, device_id={"fsdp": lax.rem(f + k, 32)}, device_id_type=MESH)
-
-    hidden = pl.ds(pl.multiple_of(half * HID, HID), HID)
+    near = [{"fsdp": zz(1) * 4 + y}, {"fsdp": zz(-1) * 4 + y}]
+    near += [{"fsdp": z * 4 + yy(k)} for k in (1, 2, 3)] + [peer(k)[1] for k in range(1, 8)]
+    for where in near:
+        pl.semaphore_signal(barrier, inc=1, device_id=where, device_id_type=MESH)
+
+    mine = pl.ds(pl.multiple_of(half * HID + odd_x * 512, 512), 1024)
     own = [
-        pltpu.make_async_copy(w_up.at[:, hidden], shard(up, 0, 0), ls.at[0]),
-        pltpu.make_async_copy(w_down.at[:, hidden], shard(down, 0, 0), ls.at[1]),
+        pltpu.make_async_copy(w_up.at[:, mine], shard(up, 0, 0), ls.at[0]),
+        pltpu.make_async_copy(w_down.at[:, mine], shard(down, 0, 0), ls.at[1]),
     ]
-    for copy in own:
+    vectors = (
+        (dw_bias_in, dw_bias), (ln_gain_in, ln_gain), (ln_bias_in, ln_bias), (b_down_in, b_down),
+        (layer_scale_in, layer_scale),
+    )
+    rows_in = [pltpu.make_async_copy(src, dst.at[0], vs.at[n]) for n, (src, dst) in enumerate(vectors)]
+    for copy in own + rows_in:
         copy.start()
     for copy in own:
         copy.wait()
-    pl.semaphore_wait(barrier, 38)
+    pl.semaphore_wait(barrier, len(near))
 
     sent = []
 
@@ -198,6 +209,29 @@
         sign = 1 - 2 * (d % 2)
         block = shard(down, d, 2 if got else -sign)
         return remote(block, block, bfs.at[d], bfr.at[d], {"fsdp": z * 4 + yy(sign)})
+
+    def x_send(buf, d, got=False):
+        sends, recvs = (xus, xur) if buf is up else (xds, xdr)
+        rows = pl.ds(pl.multiple_of(zz(d) * 192, 16), 192)
+        copies = []
+        for way in (0, 1):
+            third = (1 - odd_x if got else odd_x) * 1024 + way * 256
+            block = buf.at[rows, pl.ds(pl.multiple_of(third, 256), 256)]
+            at = way * 8 + d % 8
+            copies.append(remote(block, block, sends.at[at], recvs.at[at], x_peer(1 - 2 * way)))
+        return copies
+
+    def x_forward(buf, d):
+        for copy in x_send(buf, d):
+            send(copy)
+
+    def x_arrived(buf, d):
+        for copy in x_send(buf, d, True):
+            copy.wait_recv()
+
+    def step_down_on(d):
+        down_on(d, True).wait_recv()
+        x_forward(down, d)
 
     def step_down_z(s):
         for way in (0, 1):
@@ -219,6 +253,8 @@
             up_z(way, q, s, True).wait_recv()
             if (way, q) in up_z_steps(s + 1):
                 send(up_z(way, q, s + 1))
+        for d in (-s, s) if s < 4 else (4,):
+            x_forward(up, d)
 
     for k in (1, 3, 2):
         send(up_y(k))
@@ -235,6 +271,10 @@
     zero_rows(xp, sx)
     row_halo(xp, hs.at[0], hr.at[0], sx, "start")
 
+    step_down_z(1)
+    for copy in rows_in:
+        copy.wait()
+
     @pl.loop(0, NB)
     def _(b):
         ct = cot[:, :, lanes(b)].astype(f32).reshape(TOK, 128)
@@ -249,14 +289,19 @@
         up_y_got(k).wait_recv()
     for way, q in up_z_steps(1):
         send(up_z(way, q, 1))
-    step_down_z(1)
+    x_forward(up, 0)
     row_halo(xp, hs.at[0], hr.at[0], sx, "wait")
     pack_cols(xp, stage.at[0], sy)
     xcol = remote(stage.at[0], landed.at[0], cs.at[0], cr.at[0], {"sy": 1 - sy})
     xcol.start()
+    step_down_z(2)
     step_down_y(0)
     zero_rows(gp, sx)
     grads[84:88] = jnp.zeros((4, 8, 128), f32)
+    step_down_z(3)
+    step_down_y(7)
+    step_down_y(1)
+    step_down_on(0)
     xcol.wait()
     unpack_cols(xp, landed.at[0], sy)
 
@@ -264,8 +309,15 @@
         start = jnp.broadcast_to(dw_bias[:, lanes(b)].reshape(1, 1, 128), (ROWS, COLS, 128))
         conv[b] = depthwise(xp, b, taps, start, False).reshape(TOK, 128)
 
-    pl.loop(0, NB)(forward_conv)
-    step_down_z(2)
+    pl.loop(0, 4)(forward_conv)
+    step_up_z(1)
+    pl.loop(4, 8)(forward_conv)
+    step_down_z(4)
+    step_down_y(6)
+    step_down_y(2)
+    pl.loop(8, NB)(forward_conv)
+    step_down_on(7)
+    step_down_on(1)
 
     def over_channels(term):
         total = lax.fori_loop(0, NB, lambda b, t: t + term(b), jnp.zeros((TOK, 128), f32))
@@ -282,10 +334,9 @@
         ln[0:TOK, lanes(b)] = (normed * ln_gain[:, lanes(b)] + ln_bias[:, lanes(b)]).astype(bf16)
 
     send(tokens(ln, 1))
-    step_down_y(7)
-    step_down_y(1)
-    step_up_z(1)
-    step_down_z(3)
+    step_down_y(5)
+    step_down_y(3)
+    step_up_z(2)
     tokens(dm, 0).wait_recv()
     tokens(ln, 1).wait_recv()
 
@@ -307,25 +358,31 @@
             else:
                 pre[:, tile(n)] = pre[:, tile(n)] + term
 
+    step_down_on(6)
+    step_down_on(2)
+    step_down_y(4)
+    for d in (0, -1, 1):
+        x_arrived(up, d)
     add_pre(1)
-    step_down_y(6)
-    step_down_y(2)
-    step_up_z(2)
-    step_down_z(4)
+    step_up_z(3)
+    step_down_on(5)
+    step_down_on(3)
+    for d in (-2, 2):
+        x_arrived(up, d)
     add_pre(2)
-    step_down_y(5)
-    step_down_y(3)
-    step_up_z(3)
-    step_down_y(4)
+    step_down_on(4)
+    step_up_z(4)
+    for d in (-3, 3):
+        x_arrived(up, d)
     add_pre(3)
     for d in range(8):
-        down_on(d, True).wait_recv()
+        x_arrived(down, d)
 
     @pl.loop(0, 6)
     def _(n):
         dact[:, tile(n)] = jnp.dot(dm[...], down[:, tile(n)], preferred_element_type=f32)
 
-    step_up_z(4)
+    x_arrived(up, 4)
     add_pre(4)
 
     @pl.loop(0, 12)
@@ -482,8 +539,8 @@
         at = slice(b * 128, (b + 1) * 128)
         for i in range(KW):
             gk[i, :, at] = full[b * 7 + i, 0:7, :]
-        gg[0, at] = full[b * 7, 7, :]
-        gs[0, at] = full[b * 7 + 1, 7, :]
+        gg[at] = full[b * 7, 7, :]
+        gs[at] = full[b * 7 + 1, 7, :]
 
     for k in range(7):
         first[k].wait_send()
@@ -526,13 +583,13 @@
             jax.ShapeDtypeStruct((TOK, CHANS), bf16),
             jax.ShapeDtypeStruct((ROWS, COLS, CHANS), bf16),
             jax.ShapeDtypeStruct((KW, KW, CHANS), f32),
-            jax.ShapeDtypeStruct((1, CHANS), f32),
-            jax.ShapeDtypeStruct((1, CHANS), f32),
+            jax.ShapeDtypeStruct((CHANS,), f32),
+            jax.ShapeDtypeStruct((CHANS,), f32),
         ),
-        in_specs=[vmem] * 7 + [anywhere, vmem, anywhere, vmem, vmem],
+        in_specs=[vmem] * 4 + [anywhere] * 4 + [vmem] + [anywhere] * 3,
         out_specs=(vmem,) * 5,
         scratch_shapes=[
-            padded, padded, staged, staged, weight, weight, pair_bf16, pair_bf16,
+            *[pltpu.VMEM((1, CHANS), f32)] * 5, padded, padded, staged, staged, weight, weight, pair_bf16, pair_bf16,
             pltpu.VMEM((NB, TOK, 128), f32), pltpu.VMEM((TOK, 128), f32),
             pair_f32, pair_f32, pair_bf16, pair_bf16,
             tok_f32, tok_f32, tok_f32, tok_f32, tok_f32, tok_f32,
@@ -542,7 +599,8 @@
             pltpu.VMEM((32, 8, 128), f32),
             pltpu.VMEM((PIECE, 8, 128), f32),
             pltpu.VMEM((88, 8, 128), f32),
-            dma((2,)), dma((3,)), dma((3,)), dma((16,)), dma((16,)), dma((8,)), dma((8,)),
+            dma((2,)), dma((5,)), dma((16,)), dma((16,)), dma((16,)), dma((16,)),
+            dma((3,)), dma((3,)), dma((16,)), dma((16,)), dma((8,)), dma((8,)),
             dma((16,)), dma((16,)), dma((8,)), dma((8,)), dma((2,)), dma((2,)),
             dma((6,)), dma((6,)), dma((6,)), dma((6,)),
             dma((2, 2)), dma((2, 2)), dma((2,)), dma((2,)),
@@ -554,11 +612,11 @@
         ),
         name="block",
     )(
-        x_code[0], x_exp[0], cotangent[0], dw_kernel, row(dw_bias), row(ln_gain), row(ln_bias),
-        w_up, row(b_up), w_down.T, row(b_down), row(layer_scale),
+        x_code[0], x_exp[0], cotangent[0], dw_kernel, dw_bias, ln_gain, ln_bias,
+        w_up, row(b_up), w_down.T, b_down, layer_scale,
     )
     return (
-        block_out.reshape(1, ROWS, COLS, CHANS), grad_input[None], grad_kernel, grad_gain[0], grad_scale[0]
+        block_out.reshape(1, ROWS, COLS, CHANS), grad_input[None], grad_kernel, grad_gain, grad_scale
     )
 
 

time: 135 us -> 117 us (0.87)
  Pallas kernels: 122 us -> 110 us
  local copies, waits for them, and re-layouts: 11 us -> 6.52 us
    pallas_call x1, Pallas kernels: 122 us -> 110 us  [on_device(): pl.pallas_call(block_kernel, out_shape=(jax.ShapeDtypeStruct((TOK, CHANS)...]
    reshape x5 -> x0, local copies, waits for them, and re-layouts: 5.8 us -> none  [on_device(): row = lambda v: v.reshape(1, -1)]
    unnamed x16 -> x14, local copies, waits for them, and re-layouts: 5.19 us -> 6.52 us
where the time goes in v3:
time: 117 us
  Pallas kernels  110 us (94%)
  local copies, waits for them, and re-layouts  6.52 us (6%)
    pallas_call x1, Pallas kernels, on_device(): pl.pallas_call(block_kernel, out_shape=(jax.ShapeDtypeStruct((TOK, CHANS)...  110 us
    unnamed x14, local copies, waits for them, and re-layouts  6.52 us

profile of v3, /device:TPU:1, one launch (start us, length us, event | category | flops | bytes accessed | tf_op | source)
XLA Modules:
  0.0 116.8 jit_solution(17895584262882076964)
XLA Ops:
  0.6 1.5 %copy.17 = s32[1,8,16,12]{3,2,1,0:T(8,128)} copy(s32[1,8,16,12]{2,1,3,0:T(8,128)} %param.13) | data formatting | bytes 12288 | tf_op args[1]
  2.2 109.7 %block.1 = (bf16[128,1536]{1,0:T(8,128)(2,1)}, bf16[8,16,1536]{2,1,0:T(8,128)(2,1)}, f32[7,7,1536]{2,1,0:T(8,128)}, f32[1536]{0:T(1024)}, f32[1536]{0:T(1024)}) custom-call(bf16[8,16,1536]{2,1,0:T(8,128)(2,1)} %bitcast.7, s32[8,16,12]{2,1,0:T(8,128)} %bitcast.12, bf16[8,16,1536]{2,1,0:T(8,128)(2,1)} %bitcast.8, f32[7,7,1536]{2,1,0:T(8,128)} %taps.1, ...), custom_call_target="tpu_custom_call" | custom-call | tf_op jit(solution)/shard_map/block/pallas_call | solution.py:580
  111.8 0.0 copy-start
  111.8 1.8 %copy.23 = bf16[1,8,16,1536]{3,2,1,0:T(8,128)(2,1)} copy(bf16[1,8,16,1536]{3,2,1,0:T(8,128)(2,1)} %bitcast.10) | data formatting | bytes 786432
  113.7 0.0 copy-done
  113.7 0.0 copy-start.1
  113.7 0.7 copy.24
  114.4 0.4 copy-done.1
  114.8 0.0 copy-start.3
  114.8 0.7 copy.25
  115.5 0.0 copy-done.3
  115.5 0.0 copy-start.2
  115.5 0.6 copy.26
  116.1 0.1 copy-done.2
  116.2 0.6 copy.27
Async XLA Ops:
  111.8 1.8 %copy-start = (bf16[8,16,1536]{2,1,0:T(8,128)(2,1)S(1)}, bf16[8,16,1536]{2,1,0:T(8,128)(2,1)}, u32[]{:S(2)}) copy-start(bf16[8,16,1536]{2,1,0:T(8,128)(2,1)} %get-tuple-element.11) | copy-start | bytes 1179652
  113.7 1.1 copy-start.1
  114.8 0.7 copy-start.3
  115.5 0.7 copy-start.2

commit v4 on v3

--- a/solution.py
+++ b/solution.py
@@ -12,6 +12,21 @@
 PR, PC = 16, 32
 PIECE = 11
 HID = 1536
+MISSING_UP, MISSING_DOWN = 640, 512
+ORDER = (
+    ("uz", 0, 0, 1), ("uz", 1, 0, 1), ("uy", 1), ("uy", 3), ("uy", 2), ("tokens",), ("dz", 0, 1),
+    ("dz", 1, 1), ("dy", 0, 0), ("dy", 1, 0), ("xcols",), ("uz", 0, 0, 2), ("uz", 1, 0, 2), ("dy", 0, 7),
+    ("dy", 1, 7), ("uz", 0, 1, 1), ("uz", 1, 1, 1), ("uz", 0, 3, 1), ("uz", 1, 3, 1), ("dy", 0, 1),
+    ("dy", 1, 1), ("do", 0), ("dz", 0, 2), ("dz", 1, 2), ("uz", 0, 2, 1), ("uz", 1, 2, 1), ("unpack",),
+    ("conv", 0), ("do", 7), ("dy", 0, 6), ("uz", 0, 0, 3), ("uz", 1, 0, 3), ("conv", 3), ("do", 1),
+    ("dy", 1, 6), ("dy", 0, 2), ("uz", 0, 1, 2), ("uz", 1, 1, 2), ("conv", 6), ("dz", 0, 3), ("dz", 1, 3),
+    ("dy", 1, 2), ("uz", 0, 3, 2), ("uz", 1, 3, 2), ("conv", 9), ("do", 6), ("norm",), ("dy", 1, 5),
+    ("uz", 0, 2, 2), ("uz", 1, 2, 2), ("do", 2), ("dy", 0, 5), ("dy", 1, 3), ("uz", 0, 0, 4),
+    ("uz", 1, 1, 3), ("back", 1), ("dz", 0, 4), ("dy", 0, 3), ("uz", 0, 1, 3), ("uz", 1, 3, 3), ("pre", 1),
+    ("uz", 1, 2, 3), ("do", 5), ("dy", 0, 4), ("back", 2), ("uz", 0, 3, 3), ("do", 3), ("dy", 1, 4),
+    ("uz", 1, 3, 4), ("uz", 0, 2, 3), ("pre", 2), ("uz", 1, 2, 4), ("uz", 0, 1, 4), ("do", 4), ("back", 3),
+    ("pre", 3), ("pre", 4), ("back", 4),
+)
 GELU_C = 0.7978845608028654
 MESH = pl.DeviceIdType.MESH
 
@@ -132,7 +147,7 @@
 
     x = sy * 2 + sx // 2
     odd_x = lax.rem(x, 2)
-    window = pl.ds(pl.multiple_of(odd_x * 512, 512), 1024)
+    missing = lambda buf: MISSING_UP if buf is up else MISSING_DOWN
 
     def x_peer(sign):
         to = lax.rem(x + sign + 4, 4)
@@ -144,11 +159,11 @@
     def yy(d):
         return lax.rem(y + d + 4, 4)
 
+    def window(buf, start=0):
+        return pl.ds(pl.multiple_of(start + odd_x * missing(buf), 128), CHANS - missing(buf))
+
     def shard(buf, dz, dy):
-        return buf.at[pl.ds(pl.multiple_of((zz(dz) * 4 + yy(dy)) * 48, 16), 48), window]
-
-    def pair(buf, dz, q):
-        return buf.at[pl.ds(pl.multiple_of((zz(dz) * 4 + 2 * q) * 48, 16), 96), window]
+        return buf.at[pl.ds(pl.multiple_of((zz(dz) * 4 + yy(dy)) * 48, 16), 48), window(buf)]
 
     barrier = pltpu.get_barrier_semaphore()
     near = [{"fsdp": zz(1) * 4 + y}, {"fsdp": zz(-1) * 4 + y}]
@@ -156,10 +171,9 @@
     for where in near:
         pl.semaphore_signal(barrier, inc=1, device_id=where, device_id_type=MESH)
 
-    mine = pl.ds(pl.multiple_of(half * HID + odd_x * 512, 512), 1024)
     own = [
-        pltpu.make_async_copy(w_up.at[:, mine], shard(up, 0, 0), ls.at[0]),
-        pltpu.make_async_copy(w_down.at[:, mine], shard(down, 0, 0), ls.at[1]),
+        pltpu.make_async_copy(w_up.at[:, window(up, half * HID)], shard(up, 0, 0), ls.at[0]),
+        pltpu.make_async_copy(w_down.at[:, window(down, half * HID)], shard(down, 0, 0), ls.at[1]),
     ]
     vectors = (
         (dw_bias_in, dw_bias), (ln_gain_in, ln_gain), (ln_bias_in, ln_bias), (b_down_in, b_down),
@@ -184,14 +198,11 @@
     def up_y_got(k):
         return remote(shard(up, 0, -k), shard(up, 0, -k), a1s.at[k - 1], a1r.at[k - 1], {"fsdp": z * 4 + yy(k)})
 
-    def up_z(way, q, s, got=False):
+    def up_z(way, k, s, got=False):
         sign = 1 - 2 * way
-        block = pair(up, -sign * (s if got else s - 1), q)
-        at = way * 8 + q * 4 + s - 1
+        block = shard(up, -sign * (s if got else s - 1), -k)
+        at = way * 16 + k * 4 + s - 1
         return remote(block, block, azs.at[at], azr.at[at], {"fsdp": zz(sign) * 4 + y})
-
-    def up_z_steps(s):
-        return [(way, q) for way in (0, 1) for q in (0, 1) if s <= (4 if way == q else 3)]
 
     def down_z(way, s, got=False):
         sign = 1 - 2 * way
@@ -210,58 +221,57 @@
         block = shard(down, d, 2 if got else -sign)
         return remote(block, block, bfs.at[d], bfr.at[d], {"fsdp": z * 4 + yy(sign)})
 
-    def x_send(buf, d, got=False):
+    def x_send(buf, d, dy, got=False):
         sends, recvs = (xus, xur) if buf is up else (xds, xdr)
-        rows = pl.ds(pl.multiple_of(zz(d) * 192, 16), 192)
-        copies = []
-        for way in (0, 1):
-            third = (1 - odd_x if got else odd_x) * 1024 + way * 256
-            block = buf.at[rows, pl.ds(pl.multiple_of(third, 256), 256)]
-            at = way * 8 + d % 8
-            copies.append(remote(block, block, sends.at[at], recvs.at[at], x_peer(1 - 2 * way)))
-        return copies
-
-    def x_forward(buf, d):
-        for copy in x_send(buf, d):
-            send(copy)
-
-    def x_arrived(buf, d):
-        for copy in x_send(buf, d, True):
-            copy.wait_recv()
-
-    def step_down_on(d):
-        down_on(d, True).wait_recv()
-        x_forward(down, d)
-
-    def step_down_z(s):
-        for way in (0, 1):
-            if s <= 4 - way:
-                down_z(way, s, True).wait_recv()
-                if s + 1 <= 4 - way:
-                    send(down_z(way, s + 1))
-                d = (8 - s) if way == 0 else s
-                send(down_y(0, d))
-                send(down_y(1, d))
-
-    def step_down_y(d):
-        down_y(0, d, True).wait_recv()
-        down_y(1, d, True).wait_recv()
-        send(down_on(d))
-
-    def step_up_z(s):
-        for way, q in up_z_steps(s):
-            up_z(way, q, s, True).wait_recv()
-            if (way, q) in up_z_steps(s + 1):
-                send(up_z(way, q, s + 1))
-        for d in (-s, s) if s < 4 else (4,):
-            x_forward(up, d)
-
-    for k in (1, 3, 2):
-        send(up_y(k))
-    send(down_z(0, 1))
-    send(down_z(1, 1))
-    send(down_y(0, 0))
-    send(down_y(1, 0))
+        at = d % 8 * 4 + dy % 4
+        rows = pl.ds(pl.multiple_of((zz(d) * 4 + yy(dy)) * 48, 16), 48)
+        place = (1 - odd_x if got else odd_x) * (CHANS - missing(buf))
+        block = buf.at[rows, pl.ds(pl.multiple_of(place, 128), missing(buf))]
+        return remote(block, block, sends.at[at], recvs.at[at], x_peer(1 - 2 * ((d + dy) % 2)))
+
+    def x_arrived(buf, step):
+        for d in sorted({-step % 8, step}):
+            for dy in (0, 1, -1, 2):
+                x_send(buf, d, dy, True).wait_recv()
+
+    def handle(kind, way, k=0, s=0):
+        if kind == "uy":
+            up_y_got(way).wait_recv()
+            for to in (0, 1):
+                send(up_z(to, way, 1))
+            send(x_send(up, 0, -way))
+        elif kind == "uz":
+            up_z(way, k, s, True).wait_recv()
+            if s < (4 if way == k // 2 else 3):
+                send(up_z(way, k, s + 1))
+            send(x_send(up, s if way else -s, -k))
+        elif kind == "dz":
+            down_z(way, k, True).wait_recv()
+            if k < 4 - way:
+                send(down_z(way, k + 1))
+            d = k if way else 8 - k
+            send(down_y(0, d))
+            send(down_y(1, d))
+            send(x_send(down, d, 0))
+        elif kind == "dy":
+            down_y(way, k, True).wait_recv()
+            if k % 2 == way:
+                send(down_on(k))
+            send(x_send(down, k, 1 if way else -1))
+        else:
+            down_on(way, True).wait_recv()
+            send(x_send(down, way, 2))
+
+    send(up_y(1))
+    send(up_y(3))
+    for way in (0, 1):
+        send(up_z(way, 0, 1))
+        send(down_z(way, 1))
+    send(up_y(2))
+    for way in (0, 1):
+        send(down_y(way, 0))
+    send(x_send(up, 0, 0))
+    send(x_send(down, 0, 0))
 
     factor = jnp.left_shift(1, expo[...] + 2).astype(f32) * 0.25
     for b in range(NB):
@@ -271,74 +281,53 @@
     zero_rows(xp, sx)
     row_halo(xp, hs.at[0], hr.at[0], sx, "start")
 
-    step_down_z(1)
-    for copy in rows_in:
-        copy.wait()
-
-    @pl.loop(0, NB)
-    def _(b):
-        ct = cot[:, :, lanes(b)].astype(f32).reshape(TOK, 128)
-        dm[0:TOK, lanes(b)] = (layer_scale[:, lanes(b)] * ct).astype(bf16)
-
     def tokens(buf, at):
         return remote(buf.at[0:TOK], buf.at[TOK : 2 * TOK], ts.at[at], tr.at[at], other)
-
-    send(tokens(dm, 0))
-
-    for k in (1, 3, 2):
-        up_y_got(k).wait_recv()
-    for way, q in up_z_steps(1):
-        send(up_z(way, q, 1))
-    x_forward(up, 0)
-    row_halo(xp, hs.at[0], hr.at[0], sx, "wait")
-    pack_cols(xp, stage.at[0], sy)
-    xcol = remote(stage.at[0], landed.at[0], cs.at[0], cr.at[0], {"sy": 1 - sy})
-    xcol.start()
-    step_down_z(2)
-    step_down_y(0)
-    zero_rows(gp, sx)
-    grads[84:88] = jnp.zeros((4, 8, 128), f32)
-    step_down_z(3)
-    step_down_y(7)
-    step_down_y(1)
-    step_down_on(0)
-    xcol.wait()
-    unpack_cols(xp, landed.at[0], sy)
 
     def forward_conv(b):
         start = jnp.broadcast_to(dw_bias[:, lanes(b)].reshape(1, 1, 128), (ROWS, COLS, 128))
         conv[b] = depthwise(xp, b, taps, start, False).reshape(TOK, 128)
 
-    pl.loop(0, 4)(forward_conv)
-    step_up_z(1)
-    pl.loop(4, 8)(forward_conv)
-    step_down_z(4)
-    step_down_y(6)
-    step_down_y(2)
-    pl.loop(8, NB)(forward_conv)
-    step_down_on(7)
-    step_down_on(1)
-
-    def over_channels(term):
-        total = lax.fori_loop(0, NB, lambda b, t: t + term(b), jnp.zeros((TOK, 128), f32))
-        return jnp.sum(total, axis=1, keepdims=True) / CHANS
-
-    mu = over_channels(lambda b: conv[b])
-    var = over_channels(lambda b: (conv[b] - mu) * (conv[b] - mu))
-    rstd[...] = jnp.broadcast_to(lax.rsqrt(var + 1e-6), (TOK, 128))
-
-    @pl.loop(0, NB)
-    def _(b):
-        normed = (conv[b] - mu) * rstd[...]
-        conv[b] = normed
-        ln[0:TOK, lanes(b)] = (normed * ln_gain[:, lanes(b)] + ln_bias[:, lanes(b)]).astype(bf16)
-
-    send(tokens(ln, 1))
-    step_down_y(5)
-    step_down_y(3)
-    step_up_z(2)
-    tokens(dm, 0).wait_recv()
-    tokens(ln, 1).wait_recv()
+    xcol = remote(stage.at[0], landed.at[0], cs.at[0], cr.at[0], {"sy": 1 - sy})
+
+    def tokens_task():
+        for copy in rows_in:
+            copy.wait()
+
+        @pl.loop(0, NB)
+        def _(b):
+            ct = cot[:, :, lanes(b)].astype(f32).reshape(TOK, 128)
+            dm[0:TOK, lanes(b)] = (layer_scale[:, lanes(b)] * ct).astype(bf16)
+
+        send(tokens(dm, 0))
+        zero_rows(gp, sx)
+        grads[84:88] = jnp.zeros((4, 8, 128), f32)
+
+    def xcols_task():
+        row_halo(xp, hs.at[0], hr.at[0], sx, "wait")
+        pack_cols(xp, stage.at[0], sy)
+        xcol.start()
+
+    def unpack_task():
+        xcol.wait()
+        unpack_cols(xp, landed.at[0], sy)
+
+    def norm_task():
+        def over_channels(term):
+            total = lax.fori_loop(0, NB, lambda b, t: t + term(b), jnp.zeros((TOK, 128), f32))
+            return jnp.sum(total, axis=1, keepdims=True) / CHANS
+
+        mu = over_channels(lambda b: conv[b])
+        var = over_channels(lambda b: (conv[b] - mu) * (conv[b] - mu))
+        rstd[...] = jnp.broadcast_to(lax.rsqrt(var + 1e-6), (TOK, 128))
+
+        @pl.loop(0, NB)
+        def _(b):
+            normed = (conv[b] - mu) * rstd[...]
+            conv[b] = normed
+            ln[0:TOK, lanes(b)] = (normed * ln_gain[:, lanes(b)] + ln_bias[:, lanes(b)]).astype(bf16)
+
+        send(tokens(ln, 1))
 
     odd = lax.rem(z, 2)
 
@@ -358,32 +347,40 @@
             else:
                 pre[:, tile(n)] = pre[:, tile(n)] + term
 
-    step_down_on(6)
-    step_down_on(2)
-    step_down_y(4)
-    for d in (0, -1, 1):
-        x_arrived(up, d)
-    add_pre(1)
-    step_up_z(3)
-    step_down_on(5)
-    step_down_on(3)
-    for d in (-2, 2):
-        x_arrived(up, d)
-    add_pre(2)
-    step_down_on(4)
-    step_up_z(4)
-    for d in (-3, 3):
-        x_arrived(up, d)
-    add_pre(3)
-    for d in range(8):
-        x_arrived(down, d)
-
-    @pl.loop(0, 6)
-    def _(n):
-        dact[:, tile(n)] = jnp.dot(dm[...], down[:, tile(n)], preferred_element_type=f32)
-
-    x_arrived(up, 4)
-    add_pre(4)
+    def add_dact(s):
+        base = (-odd, -2 + 3 * odd, 2 - 5 * odd, 4 - odd)[s - 1]
+        rows = pl.ds(pl.multiple_of(zz(base) * 192, 384), 384)
+
+        @pl.loop(0, 6)
+        def _(n):
+            term = jnp.dot(dm[:, rows], down[rows, tile(n)], preferred_element_type=f32)
+            dact[:, tile(n)] = term if s == 1 else dact[:, tile(n)] + term
+
+    for name, *rest in ORDER:
+        if name == "tokens":
+            tokens_task()
+        elif name == "xcols":
+            xcols_task()
+        elif name == "unpack":
+            unpack_task()
+        elif name == "conv":
+            pl.loop(rest[0], rest[0] + 3)(forward_conv)
+        elif name == "norm":
+            norm_task()
+        elif name == "pre":
+            if rest[0] == 1:
+                tokens(ln, 1).wait_recv()
+                x_arrived(up, 0)
+            x_arrived(up, rest[0])
+            add_pre(rest[0])
+        elif name == "back":
+            if rest[0] == 1:
+                tokens(dm, 0).wait_recv()
+                x_arrived(down, 0)
+            x_arrived(down, rest[0])
+            add_dact(rest[0])
+        else:
+            handle(name, *rest)
 
     @pl.loop(0, 12)
     def _(n):
@@ -438,6 +435,15 @@
 
     row_halo(gp, hs.at[1], hr.at[1], sx, "start")
 
+    @pl.loop(0, 8)
+    def _(b):
+        kernel_grad(xp, gp, grads, b)
+
+    row_halo(gp, hs.at[1], hr.at[1], sx, "wait")
+    pack_cols(gp, stage.at[1], sy)
+    col = remote(stage.at[1], landed.at[1], cs.at[1], cr.at[1], {"sy": 1 - sy})
+    col.start()
+
     @pl.loop(0, NB)
     def _(b):
         @pl.when(lax.rem(b, 2) == 0)
@@ -452,16 +458,7 @@
         for i in range(2, 7):
             grads[b * 7 + i, 7, :] = jnp.zeros((128,), jnp.float32)
 
-    @pl.loop(0, 6)
-    def _(b):
-        kernel_grad(xp, gp, grads, b)
-
-    row_halo(gp, hs.at[1], hr.at[1], sx, "wait")
-    pack_cols(gp, stage.at[1], sy)
-    col = remote(stage.at[1], landed.at[1], cs.at[1], cr.at[1], {"sy": 1 - sy})
-    col.start()
-
-    @pl.loop(6, NB)
+    @pl.loop(8, NB)
     def _(b):
         kernel_grad(xp, gp, grads, b)
 
@@ -599,8 +596,8 @@
             pltpu.VMEM((32, 8, 128), f32),
             pltpu.VMEM((PIECE, 8, 128), f32),
             pltpu.VMEM((88, 8, 128), f32),
-            dma((2,)), dma((5,)), dma((16,)), dma((16,)), dma((16,)), dma((16,)),
-            dma((3,)), dma((3,)), dma((16,)), dma((16,)), dma((8,)), dma((8,)),
+            dma((2,)), dma((5,)), dma((32,)), dma((32,)), dma((32,)), dma((32,)),
+            dma((3,)), dma((3,)), dma((32,)), dma((32,)), dma((8,)), dma((8,)),
             dma((16,)), dma((16,)), dma((8,)), dma((8,)), dma((2,)), dma((2,)),
             dma((6,)), dma((6,)), dma((6,)), dma((6,)),
             dma((2, 2)), dma((2, 2)), dma((2,)), dma((2,)),

time: 117 us -> 112 us (0.957)
  Pallas kernels: 110 us -> 104 us
    pallas_call x1, Pallas kernels: 110 us -> 104 us  [on_device(): pl.pallas_call(block_kernel, out_shape=(jax.ShapeDtypeStruct((TOK, CHANS)...]
where the time goes in v4:
time: 112 us; the launch traced here: 111 us
  Pallas kernels  104 us (93%)
  local copies, waits for them, and re-layouts  6.52 us (6%)
    pallas_call x1, Pallas kernels, on_device(): pl.pallas_call(block_kernel, out_shape=(jax.ShapeDtypeStruct((TOK, CHANS)...  104 us
    unnamed x14, local copies, waits for them, and re-layouts  6.52 us

profile of v4, /device:TPU:1, one launch (start us, length us, event | category | flops | bytes accessed | tf_op | source)
XLA Modules:
  0.0 111.3 jit_solution(4870709358201525061)
XLA Ops:
  0.6 1.5 %copy.17 = s32[1,8,16,12]{3,2,1,0:T(8,128)} copy(s32[1,8,16,12]{2,1,3,0:T(8,128)} %param.13) | data formatting | bytes 12288 | tf_op args[1]
  2.2 104.1 %block.1 = (bf16[128,1536]{1,0:T(8,128)(2,1)}, bf16[8,16,1536]{2,1,0:T(8,128)(2,1)}, f32[7,7,1536]{2,1,0:T(8,128)}, f32[1536]{0:T(1024)}, f32[1536]{0:T(1024)}) custom-call(bf16[8,16,1536]{2,1,0:T(8,128)(2,1)} %bitcast.7, s32[8,16,12]{2,1,0:T(8,128)} %bitcast.12, bf16[8,16,1536]{2,1,0:T(8,128)(2,1)} %bitcast.8, f32[7,7,1536]{2,1,0:T(8,128)} %taps.1, ...), custom_call_target="tpu_custom_call" | custom-call | tf_op jit(solution)/shard_map/block/pallas_call | solution.py:577
  106.3 0.0 copy-start
  106.3 1.8 %copy.23 = bf16[1,8,16,1536]{3,2,1,0:T(8,128)(2,1)} copy(bf16[1,8,16,1536]{3,2,1,0:T(8,128)(2,1)} %bitcast.10) | data formatting | bytes 786432
  108.1 0.0 copy-done
  108.1 0.0 copy-start.1
  108.1 0.7 copy.24
  108.9 0.4 copy-done.1
  109.2 0.0 copy-start.3
  109.2 0.7 copy.25
  110.0 0.0 copy-done.3
  110.0 0.0 copy-start.2
  110.0 0.6 copy.26
  110.6 0.1 copy-done.2
  110.7 0.6 copy.27
Async XLA Ops:
  106.3 1.8 %copy-start = (bf16[8,16,1536]{2,1,0:T(8,128)(2,1)S(1)}, bf16[8,16,1536]{2,1,0:T(8,128)(2,1)}, u32[]{:S(2)}) copy-start(bf16[8,16,1536]{2,1,0:T(8,128)(2,1)} %get-tuple-element.11) | copy-start | bytes 1179652
  108.1 1.1 %copy-start.1 = (f32[7,7,1536]{2,1,0:T(8,128)S(1)}, f32[7,7,1536]{2,1,0:T(8,128)}, u32[]{:S(2)}) copy-start(f32[7,7,1536]{2,1,0:T(8,128)} %get-tuple-element.22) | copy-start | bytes 903172
  109.2 0.7 copy-start.3
  110.0 0.7 copy-start.2

commit v5 on v4

--- a/solution.py
+++ b/solution.py
@@ -273,10 +273,10 @@
     send(x_send(up, 0, 0))
     send(x_send(down, 0, 0))
 
-    factor = jnp.left_shift(1, expo[...] + 2).astype(f32) * 0.25
     for b in range(NB):
         at = slice(b * 128, (b + 1) * 128)
-        scaled = code[:, :, at].astype(f32) * factor[:, :, b : b + 1]
+        factor = jnp.left_shift(1, expo[b] + 2).astype(f32) * 0.25
+        scaled = code[:, :, at].astype(f32) * factor[:, :, None]
         xp[b, 3:11, 8:24, :] = scaled
     zero_rows(xp, sx)
     row_halo(xp, hs.at[0], hr.at[0], sx, "start")
@@ -395,27 +395,30 @@
     moved_dln = (send_dln, got_dln, dls, dlr)
     moved_mlp = (send_mlp, got_mlp, mls, mlr)
 
+    def wide(n):
+        return pl.ds(pl.multiple_of(n * 512, 512), 512)
+
     def arrived(moved, n):
         src, dst, sends, recvs = moved
-        return remote(src.at[:, tile(n)], dst.at[:, tile(n)], sends.at[n], recvs.at[n], other)
+        return remote(src.at[:, wide(n)], dst.at[:, wide(n)], sends.at[n], recvs.at[n], other)
 
     def down_projection(lhs, weights, mine, moved):
-        @pl.loop(0, 6)
+        @pl.loop(0, 3)
         def _(n):
             out = lax.dot_general(
-                lhs[...], weights[tile(n), :], (((1,), (1,)), ((), ())), preferred_element_type=f32
+                lhs[...], weights[wide(n), :], (((1,), (1,)), ((), ())), preferred_element_type=f32
             )
-            mine[:, tile(n)] = out[0:TOK]
-            moved[0][:, tile(n)] = out[TOK : 2 * TOK]
+            mine[:, wide(n)] = out[0:TOK]
+            moved[0][:, wide(n)] = out[TOK : 2 * TOK]
             arrived(moved, n).start()
 
     down_projection(dpre, up, mine_dln, moved_dln)
     down_projection(act, down, mine_mlp, moved_mlp)
 
     def back_sums(b, sums):
-        @pl.when(lax.rem(b, 2) == 0)
-        def _():
-            arrived(moved_dln, b // 2).wait_recv()
+        @pl.when(lax.rem(b, 4) == 0)
+        def _():
+            arrived(moved_dln, b // 4).wait_recv()
 
         d_ln = mine_dln[:, lanes(b)] + got_dln[:, lanes(b)]
         grads[b * 7, 7, :] = jnp.sum(d_ln * conv[b], axis=0)
@@ -446,9 +449,9 @@
 
     @pl.loop(0, NB)
     def _(b):
-        @pl.when(lax.rem(b, 2) == 0)
-        def _():
-            arrived(moved_mlp, b // 2).wait_recv()
+        @pl.when(lax.rem(b, 4) == 0)
+        def _():
+            arrived(moved_mlp, b // 4).wait_recv()
 
         mlp = (mine_mlp[:, lanes(b)] + got_mlp[:, lanes(b)]) + b_down[:, lanes(b)]
         ct = cot[:, :, lanes(b)].astype(jnp.float32).reshape(TOK, 128)
@@ -554,7 +557,7 @@
         def _(k):
             spread(k).wait_send()
 
-    for n in range(6):
+    for n in range(3):
         arrived(moved_dln, n).wait_send()
         arrived(moved_mlp, n).wait_send()
     for copy in sent:
@@ -609,7 +612,7 @@
         ),
         name="block",
     )(
-        x_code[0], x_exp[0], cotangent[0], dw_kernel, dw_bias, ln_gain, ln_bias,
+        x_code[0], x_exp[0].transpose(2, 0, 1), cotangent[0], dw_kernel, dw_bias, ln_gain, ln_bias,
         w_up, row(b_up), w_down.T, b_down, layer_scale,
     )
     return (

time: 112 us -> 109 us (0.973)
  local copies, waits for them, and re-layouts: 6.52 us -> 4.97 us
    unnamed x14 -> x13, local copies, waits for them, and re-layouts: 6.52 us -> 4.97 us
where the time goes in v5:
time: 109 us
  Pallas kernels  103 us (94%)
  local copies, waits for them, and re-layouts  4.97 us (5%)
    pallas_call x1, Pallas kernels, on_device(): pl.pallas_call(block_kernel, out_shape=(jax.ShapeDtypeStruct((TOK, CHANS)...  103 us
    unnamed x13, local copies, waits for them, and re-layouts  4.97 us

profile of v5, /device:TPU:1, one launch (start us, length us, event | category | flops | bytes accessed | tf_op | source)
XLA Modules:
  0.0 108.7 jit_solution(3945956225194774509)
XLA Ops:
  0.6 103.0 %block.1 = (bf16[128,1536]{1,0:T(8,128)(2,1)}, bf16[8,16,1536]{2,1,0:T(8,128)(2,1)}, f32[7,7,1536]{2,1,0:T(8,128)}, f32[1536]{0:T(1024)}, f32[1536]{0:T(1024)}) custom-call(bf16[8,16,1536]{2,1,0:T(8,128)(2,1)} %bitcast.9, s32[12,8,16]{2,1,0:T(8,128)} %bitcast.14, bf16[8,16,1536]{2,1,0:T(8,128)(2,1)} %bitcast.10, f32[7,7,1536]{2,1,0:T(8,128)} %taps.1, ...), custom_call_target="tpu_custom_call" | custom-call | tf_op jit(solution)/shard_map/block/pallas_call | solution.py:580
  103.7 0.0 copy-start
  103.7 1.8 %copy.22 = bf16[1,8,16,1536]{3,2,1,0:T(8,128)(2,1)} copy(bf16[1,8,16,1536]{3,2,1,0:T(8,128)(2,1)} %bitcast.12) | data formatting | bytes 786432
  105.5 0.0 copy-done
  105.5 0.0 copy-start.1
  105.5 0.7 copy.23
  106.2 0.4 copy-done.1
  106.6 0.0 copy-start.3
  106.6 0.7 copy.24
  107.3 0.0 copy-done.3
  107.4 0.0 copy-start.2
  107.4 0.6 copy.25
  108.0 0.1 copy-done.2
  108.1 0.6 copy.26
Async XLA Ops:
  103.7 1.8 %copy-start = (bf16[8,16,1536]{2,1,0:T(8,128)(2,1)S(1)}, bf16[8,16,1536]{2,1,0:T(8,128)(2,1)}, u32[]{:S(2)}) copy-start(bf16[8,16,1536]{2,1,0:T(8,128)(2,1)} %get-tuple-element.11) | copy-start | bytes 1179652
  105.5 1.1 %copy-start.1 = (f32[7,7,1536]{2,1,0:T(8,128)S(1)}, f32[7,7,1536]{2,1,0:T(8,128)}, u32[]{:S(2)}) copy-start(f32[7,7,1536]{2,1,0:T(8,128)} %get-tuple-element.22) | copy-start | bytes 903172
  106.6 0.7 copy-start.3
  107.4 0.7 copy-start.2

commit v6 on v5

--- a/solution.py
+++ b/solution.py
@@ -331,30 +331,30 @@
 
     odd = lax.rem(z, 2)
 
-    def tile(n):
-        return pl.ds(pl.multiple_of(n * 256, 256), 256)
+    def wide(n):
+        return pl.ds(pl.multiple_of(n * 512, 512), 512)
 
     def add_pre(s):
         base = (-odd, -2 + 3 * odd, 2 - 5 * odd, 4 - odd)[s - 1]
         rows = pl.ds(pl.multiple_of(zz(base) * 192, 384), 384)
 
-        @pl.loop(0, 6)
+        @pl.loop(0, 3)
         def _(n):
-            term = jnp.dot(ln[:, rows], up[rows, tile(n)], preferred_element_type=f32)
+            term = jnp.dot(ln[:, rows], up[rows, wide(n)], preferred_element_type=f32)
             if s == 1:
-                start = pl.multiple_of(half * HID + n * 256, 256)
-                pre[:, tile(n)] = term + b_up[:, pl.ds(start, 256)]
+                start = pl.multiple_of(half * HID + n * 512, 512)
+                pre[:, wide(n)] = term + b_up[:, pl.ds(start, 512)]
             else:
-                pre[:, tile(n)] = pre[:, tile(n)] + term
+                pre[:, wide(n)] = pre[:, wide(n)] + term
 
     def add_dact(s):
         base = (-odd, -2 + 3 * odd, 2 - 5 * odd, 4 - odd)[s - 1]
         rows = pl.ds(pl.multiple_of(zz(base) * 192, 384), 384)
 
-        @pl.loop(0, 6)
+        @pl.loop(0, 3)
         def _(n):
-            term = jnp.dot(dm[:, rows], down[rows, tile(n)], preferred_element_type=f32)
-            dact[:, tile(n)] = term if s == 1 else dact[:, tile(n)] + term
+            term = jnp.dot(dm[:, rows], down[rows, wide(n)], preferred_element_type=f32)
+            dact[:, wide(n)] = term if s == 1 else dact[:, wide(n)] + term
 
     for name, *rest in ORDER:
         if name == "tokens":
@@ -394,9 +394,6 @@
 
     moved_dln = (send_dln, got_dln, dls, dlr)
     moved_mlp = (send_mlp, got_mlp, mls, mlr)
-
-    def wide(n):
-        return pl.ds(pl.multiple_of(n * 512, 512), 512)
 
     def arrived(moved, n):
         src, dst, sends, recvs = moved

time: 109 us -> 108 us (level)
    pallas_call x1, Pallas kernels: 103 us -> 102 us  [on_device(): pl.pallas_call(block_kernel, out_shape=(jax.ShapeDtypeStruct((TOK, CHANS)...]
where the time goes in v6:
time: 108 us; the launch traced here: 107 us
  Pallas kernels  102 us (94%)
  local copies, waits for them, and re-layouts  4.97 us (5%)
    pallas_call x1, Pallas kernels, on_device(): pl.pallas_call(block_kernel, out_shape=(jax.ShapeDtypeStruct((TOK, CHANS)...  102 us
    unnamed x13, local copies, waits for them, and re-layouts  4.97 us

profile of v6, /device:TPU:1, one launch (start us, length us, event | category | flops | bytes accessed | tf_op | source)
XLA Modules:
  0.0 107.3 jit_solution(8729061278057462663)
XLA Ops:
  0.6 101.6 %block.1 = (bf16[128,1536]{1,0:T(8,128)(2,1)}, bf16[8,16,1536]{2,1,0:T(8,128)(2,1)}, f32[7,7,1536]{2,1,0:T(8,128)}, f32[1536]{0:T(1024)}, f32[1536]{0:T(1024)}) custom-call(bf16[8,16,1536]{2,1,0:T(8,128)(2,1)} %bitcast.9, s32[12,8,16]{2,1,0:T(8,128)} %bitcast.14, bf16[8,16,1536]{2,1,0:T(8,128)(2,1)} %bitcast.10, f32[7,7,1536]{2,1,0:T(8,128)} %taps.1, ...), custom_call_target="tpu_custom_call" | custom-call | tf_op jit(solution)/shard_map/block/pallas_call | solution.py:577
  102.3 0.0 copy-start
  102.3 1.8 %copy.22 = bf16[1,8,16,1536]{3,2,1,0:T(8,128)(2,1)} copy(bf16[1,8,16,1536]{3,2,1,0:T(8,128)(2,1)} %bitcast.12) | data formatting | bytes 786432
  104.1 0.0 copy-done
  104.1 0.0 copy-start.1
  104.1 0.7 copy.23
  104.9 0.4 copy-done.1
  105.2 0.0 copy-start.3
  105.2 0.7 copy.24
  106.0 0.0 copy-done.3
  106.0 0.0 copy-start.2
  106.0 0.6 copy.25
  106.6 0.1 copy-done.2
  106.7 0.6 copy.26
Async XLA Ops:
  102.3 1.8 %copy-start = (bf16[8,16,1536]{2,1,0:T(8,128)(2,1)S(1)}, bf16[8,16,1536]{2,1,0:T(8,128)(2,1)}, u32[]{:S(2)}) copy-start(bf16[8,16,1536]{2,1,0:T(8,128)(2,1)} %get-tuple-element.11) | copy-start | bytes 1179652
  104.1 1.1 %copy-start.1 = (f32[7,7,1536]{2,1,0:T(8,128)S(1)}, f32[7,7,1536]{2,1,0:T(8,128)}, u32[]{:S(2)}) copy-start(f32[7,7,1536]{2,1,0:T(8,128)} %get-tuple-element.22) | copy-start | bytes 903172
  105.2 0.7 copy-start.3
  106.0 0.7 copy-start.2

commit v7 on v6

--- a/solution.py
+++ b/solution.py
@@ -334,27 +334,30 @@
     def wide(n):
         return pl.ds(pl.multiple_of(n * 512, 512), 512)
 
+    def broad(n):
+        return pl.ds(pl.multiple_of(n * 768, 256), 768)
+
     def add_pre(s):
         base = (-odd, -2 + 3 * odd, 2 - 5 * odd, 4 - odd)[s - 1]
         rows = pl.ds(pl.multiple_of(zz(base) * 192, 384), 384)
 
-        @pl.loop(0, 3)
+        @pl.loop(0, 2)
         def _(n):
-            term = jnp.dot(ln[:, rows], up[rows, wide(n)], preferred_element_type=f32)
+            term = jnp.dot(ln[:, rows], up[rows, broad(n)], preferred_element_type=f32)
             if s == 1:
-                start = pl.multiple_of(half * HID + n * 512, 512)
-                pre[:, wide(n)] = term + b_up[:, pl.ds(start, 512)]
+                start = pl.multiple_of(half * HID + n * 768, 256)
+                pre[:, broad(n)] = term + b_up[:, pl.ds(start, 768)]
             else:
-                pre[:, wide(n)] = pre[:, wide(n)] + term
+                pre[:, broad(n)] = pre[:, broad(n)] + term
 
     def add_dact(s):
         base = (-odd, -2 + 3 * odd, 2 - 5 * odd, 4 - odd)[s - 1]
         rows = pl.ds(pl.multiple_of(zz(base) * 192, 384), 384)
 
-        @pl.loop(0, 3)
+        @pl.loop(0, 2)
         def _(n):
-            term = jnp.dot(dm[:, rows], down[rows, wide(n)], preferred_element_type=f32)
-            dact[:, wide(n)] = term if s == 1 else dact[:, wide(n)] + term
+            term = jnp.dot(dm[:, rows], down[rows, broad(n)], preferred_element_type=f32)
+            dact[:, broad(n)] = term if s == 1 else dact[:, broad(n)] + term
 
     for name, *rest in ORDER:
         if name == "tokens":

time: 108 us -> 107 us (level)
  no operation moved by 1% of the time
where the time goes in v7:
time: 107 us
  Pallas kernels  101 us (94%)
  local copies, waits for them, and re-layouts  4.97 us (5%)
    pallas_call x1, Pallas kernels, on_device(): pl.pallas_call(block_kernel, out_shape=(jax.ShapeDtypeStruct((TOK, CHANS)...  101 us
    unnamed x13, local copies, waits for them, and re-layouts  4.97 us

profile of v7, /device:TPU:1, one launch (start us, length us, event | category | flops | bytes accessed | tf_op | source)
XLA Modules:
  0.0 106.8 jit_solution(5182821551428160496)
XLA Ops:
  0.6 101.1 %block.1 = (bf16[128,1536]{1,0:T(8,128)(2,1)}, bf16[8,16,1536]{2,1,0:T(8,128)(2,1)}, f32[7,7,1536]{2,1,0:T(8,128)}, f32[1536]{0:T(1024)}, f32[1536]{0:T(1024)}) custom-call(bf16[8,16,1536]{2,1,0:T(8,128)(2,1)} %bitcast.9, s32[12,8,16]{2,1,0:T(8,128)} %bitcast.14, bf16[8,16,1536]{2,1,0:T(8,128)(2,1)} %bitcast.10, f32[7,7,1536]{2,1,0:T(8,128)} %taps.1, ...), custom_call_target="tpu_custom_call" | custom-call | tf_op jit(solution)/shard_map/block/pallas_call | solution.py:580
  101.8 0.0 copy-start
  101.8 1.8 %copy.22 = bf16[1,8,16,1536]{3,2,1,0:T(8,128)(2,1)} copy(bf16[1,8,16,1536]{3,2,1,0:T(8,128)(2,1)} %bitcast.12) | data formatting | bytes 786432
  103.6 0.0 copy-done
  103.6 0.0 copy-start.1
  103.6 0.7 copy.23
  104.4 0.4 copy-done.1
  104.7 0.0 copy-start.3
  104.7 0.7 copy.24
  105.5 0.0 copy-done.3
  105.5 0.0 copy-start.2
  105.5 0.6 copy.25
  106.1 0.1 copy-done.2
  106.2 0.6 copy.26
Async XLA Ops:
  101.8 1.8 %copy-start = (bf16[8,16,1536]{2,1,0:T(8,128)(2,1)S(1)}, bf16[8,16,1536]{2,1,0:T(8,128)(2,1)}, u32[]{:S(2)}) copy-start(bf16[8,16,1536]{2,1,0:T(8,128)(2,1)} %get-tuple-element.11) | copy-start | bytes 1179652
  103.6 1.1 %copy-start.1 = (f32[7,7,1536]{2,1,0:T(8,128)S(1)}, f32[7,7,1536]{2,1,0:T(8,128)}, u32[]{:S(2)}) copy-start(f32[7,7,1536]{2,1,0:T(8,128)} %get-tuple-element.22) | copy-start | bytes 903172
  104.7 0.7 copy-start.3
  105.5 0.7 copy-start.2
